TPU v7x, 512 devices: a whole 4x8x8 slice. The times are simulated.
512 devices in a mesh: tok: 64 (over x, y, z_lo), pan: 8 (over z_hi, core).
Axes of the slice: x: 4, y: 8, z: 8 (z_hi: 4, z_lo: 2; z = z_hi * 2 + z_lo), core: 2. Of those that a mesh axis runs over, the one named last changes fastest.
Arguments:
- student: bfloat16 [32768, 16384], P('tok', 'pan'), may hold values from -6 to 6
- teacher: bfloat16 [32768, 16384], P('tok', 'pan'), may hold values from -6 to 6
- weight_panel: bfloat16 [16384, 128], P('pan'), may hold values from -6 to 6
Outputs:
- corrected: float32 [16384, 128], P(('pan', 'tok'))
- mismatch: float32 [32768, 128], P('tok')
All inputs are finite; a program needn't handle non-finite values.
Results may differ from a plain program's by a relative error of at most 0.0055.
Values may be sent and summed in bfloat16 or wider, within the bound.
No kernel may reach another device: no remote copies, remote signals or barrier semaphores. Data moves between devices by JAX's collectives and lax.ppermute only.
A program may use at most 64 MiB of HBM per device.

v0:
```python
import math

import jax
import jax.numpy as jnp
from jax import lax
from jax.sharding import PartitionSpec as P

D = 16384
ITERS = 2


def local(student, teacher, weight_panel):
    tok_count = lax.axis_size("tok")
    block_rows = student.shape[1]
    rows = block_rows // tok_count
    scale = 1.0 / math.sqrt(D)
    coef = 0.25 * math.sqrt(D) / (student.shape[0] * tok_count)
    teacher_part = jnp.dot(teacher, weight_panel, preferred_element_type=jnp.float32)
    student_part = jnp.dot(student, weight_panel, preferred_element_type=jnp.float32)
    teacher_sum, student_sum = lax.psum((teacher_part, student_part), "pan")
    target = teacher_sum * scale
    mismatch = target - student_sum * scale
    first_row = lax.axis_index("tok") * rows
    owned = lax.dynamic_slice_in_dim(weight_panel, first_row, rows, 0).astype(jnp.float32)
    for step in range(ITERS):
        rounded = mismatch.astype(jnp.bfloat16)
        share = lax.psum_scatter(
            lax.dot_general(
                student, rounded, (((0,), (0,)), ((), ())), preferred_element_type=jnp.float32
            ),
            "tok",
            scatter_dimension=0,
            tiled=True,
        )
        owned = owned + coef * share
        partial_proj = jnp.dot(
            student,
            lax.all_gather(owned.astype(jnp.bfloat16), "tok", axis=0, tiled=True),
            preferred_element_type=jnp.float32,
        )
        student_sum = lax.psum(partial_proj, "pan")
        mismatch = target - student_sum * scale
    return (owned, mismatch)


def solution(mesh):
    in_specs = (P("tok", "pan"), P("tok", "pan"), P("pan", None))
    out_specs = (P(("pan", "tok"), None), P("tok", None))
    return jax.shard_map(local, mesh=mesh, in_specs=in_specs, out_specs=out_specs, check_vma=False)
```

profile of v0, /device:TPU:1, one launch (start us, length us, event | category | flops | bytes accessed | tf_op | source)
XLA Modules:
  0.0 1199.4 jit_solution(17082311907777503014)
XLA Ops:
  7.2 0.0 copy-start
  7.2 0.0 copy-start.2
  7.2 0.0 all-reduce.9.cloned.1.call-start
  7.2 3.2 fusion.6
  10.5 0.0 copy-done
  10.5 0.0 copy-done.2
  10.5 1.4 fusion.7
  11.9 0.0 all-reduce.9.cloned.1.call-update
  11.9 0.0 reduce-scatter.7.cloned.1.call-start
  12.0 84.5 %all-reduce.9.cloned.1.call-done = (f32[512,128]{1,0:T(8,128)}, f32[512,128]{1,0:T(8,128)}) async-done(((f32[512,128]{1,0:T(8,128)}, f32[512,128]{1,0:T(8,128)}), (f32[512,128]{1,0:T(8,128)}, f32[512,128]{1,0:T(8,128)})) %all-reduce.9.cloned.1.call-update) | async-done | bytes 524304 | tf_op jit(solution)/shard_map/psum | solution.py:20
  96.5 1.5 convolution_bitcast_fusion.1
  98.0 1.3 copy.14
  99.3 0.0 reduce-scatter.7.cloned.1.call-update
  99.3 0.0 copy-start.1
  99.4 0.0 all-reduce.5.cloned.1.call-start
  99.4 0.7 constant_dynamic-slice_fusion
  100.1 0.1 copy.18
  100.3 264.7 %reduce-scatter.7.cloned.1.call-done = f32[32,128]{1,0:T(8,128)} async-done(((f32[2048,128]{1,0:T(8,128)}), f32[32,128]{1,0:T(8,128)}) %reduce-scatter.7.cloned.1.call-update) | async-done | bytes 16400
  364.9 0.8 copy.15
  365.8 0.1 copy.9
  365.8 126.6 %all_gather.6 = bf16[2048,128]{1,0:T(8,128)(2,1)S(1)} all-gather(bf16[32,128]{1,0:T(8,128)(2,1)S(1)} %copy.9), channel_id=1, replica_groups=mesh['tok'=64,'pan'=8] {'tok'}, dimensions={0}, use_global_device_ids=true | all-gather | bytes 532480 | tf_op jit(solution)/shard_map/all_gather | solution.py:38
  492.5 1.4 convolution_bitcast_fusion.3
  493.9 0.0 all-reduce.5.cloned.1.call-update
  493.9 0.0 reduce-scatter.9.cloned.1.call-start
  493.9 150.0 %all-reduce.5.cloned.1.call-done = f32[512,128]{1,0:T(8,128)} async-done(((f32[512,128]{1,0:T(8,128)}), f32[512,128]{1,0:T(8,128)}) %all-reduce.5.cloned.1.call-update) | async-done | bytes 262160 | tf_op jit(solution)/shard_map/psum | solution.py:41
  643.9 0.0 copy-done.1
  643.9 1.4 convolution_bitcast_fusion
  645.4 1.3 copy.16
  646.7 0.0 reduce-scatter.9.cloned.1.call-update
  646.7 0.0 all-reduce.7.cloned.1.call-start
  646.8 265.9 %reduce-scatter.9.cloned.1.call-done = f32[32,128]{1,0:T(8,128)} async-done(((f32[2048,128]{1,0:T(8,128)}), f32[32,128]{1,0:T(8,128)}) %reduce-scatter.9.cloned.1.call-update) | async-done | bytes 16400
  912.6 0.8 copy.17
  913.5 0.1 copy.10
  913.6 126.8 %all_gather.7 = bf16[2048,128]{1,0:T(8,128)(2,1)S(1)} all-gather(bf16[32,128]{1,0:T(8,128)(2,1)S(1)} %copy.10), channel_id=1, replica_groups=mesh['tok'=64,'pan'=8] {'tok'}, dimensions={0}, use_global_device_ids=true | all-gather | bytes 532480 | tf_op jit(solution)/shard_map/all_gather | solution.py:38
  1040.3 1.4 convolution_bitcast_fusion.2
  1041.8 0.0 all-reduce.7.cloned.1.call-update
  1041.8 0.7 copy.12
  1042.5 148.8 %all-reduce.7.cloned.1.call-done = f32[512,128]{1,0:T(8,128)} async-done(((f32[512,128]{1,0:T(8,128)}), f32[512,128]{1,0:T(8,128)}) %all-reduce.7.cloned.1.call-update) | async-done | bytes 262160 | tf_op jit(solution)/shard_map/psum | solution.py:41
  1191.2 1.7 multiply_subtract_fusion
  (2 shorter events, 0.0 us)
Async XLA Ops:
  7.2 3.3 copy-start
  7.2 3.3 copy-start.2
  7.2 89.3 %all-reduce.9.cloned.1.call-start = ((), (), s32[]{:S(2)}) async-start(), calls=%async_computation.6 | async-start | bytes 1048576 | tf_op jit(solution)/shard_map/psum | solution.py:20
  11.9 353.0 %reduce-scatter.7.cloned.1.call-start = ((), (), s32[]{:S(2)}) async-start(), calls=%async_computation.4 | async-start | bytes 1064960
  99.3 544.6 %copy-start.1 = (f32[512,128]{1,0:T(8,128)S(1)}, f32[512,128]{1,0:T(8,128)}, u32[]{:S(2)}) copy-start(f32[512,128]{1,0:T(8,128)} %get-tuple-element.7) | copy-start | bytes 786436
  99.4 544.6 %all-reduce.5.cloned.1.call-start = ((), (), s32[]{:S(2)}) async-start(), calls=%async_computation.2 | async-start | bytes 524288 | tf_op jit(solution)/shard_map/psum | solution.py:41
  493.9 418.8 %reduce-scatter.9.cloned.1.call-start = ((), (), s32[]{:S(2)}) async-start(), calls=%async_computation.5 | async-start | bytes 1064960
  646.7 544.5 %all-reduce.7.cloned.1.call-start = ((), (), s32[]{:S(2)}) async-start(), calls=%async_computation.3 | async-start | bytes 524288 | tf_op jit(solution)/shard_map/psum | solution.py:41
Sparse Core Ops, SparseCore 0:
  12.0 84.4 all-reduce.8
  99.5 265.3 reduce-scatter.6
  494.0 149.8 all-reduce.4
  646.8 265.7 reduce-scatter.8
  1041.9 149.2 all-reduce.6
where the time goes:
time: 1200 us
  waiting for transfers between devices  914 us (76%)
  blocking collectives  253 us (21%)
  between operations  13.8 us (1%)
    unnamed x7, waiting for transfers between devices  531 us
    psum x2, waiting for transfers between devices, local(): student_sum = lax.psum(partial_proj, 'pan')  299 us
    all_gather x2, blocking collectives, local(): lax.all_gather(owned.astype(jnp.bfloat16), 'tok', axis=0, tiled=True)  253 us
    psum x1, waiting for transfers between devices, local(): teacher_sum, student_sum = lax.psum((teacher_part, student_part), 'pan')  84.5 us
  transfers between devices with their start and end apart: 5, of which 5 were waited for; matrix products, arithmetic and copies ran while one was open for 0% of the time, Pallas kernels for 0%

commit v1 on v0

v1 whole, which is shorter than its diff:
```python
import math

import jax
import jax.numpy as jnp
from jax import lax
from jax.sharding import PartitionSpec as P

D = 16384
ITERS = 2


def exchange(blocks, axis):
    return lax.all_to_all(blocks, axis, 0, 0, tiled=True)


def spread(own, axis):
    count = lax.axis_size(axis)
    everywhere = jnp.broadcast_to(own[None], (count,) + own.shape)
    got = exchange(everywhere, axis)
    return got.reshape((count * own.shape[0],) + own.shape[1:])


def reduce_rows(partial, axis):
    count = lax.axis_size(axis)
    blocks = partial.astype(jnp.bfloat16).reshape((count, -1) + partial.shape[1:])
    return jnp.sum(exchange(blocks, axis).astype(jnp.float32), axis=0)


def local(student, teacher, weight_panel):
    tok_count = lax.axis_size("tok")
    rows = student.shape[1] // tok_count
    scale = 1.0 / math.sqrt(D)
    coef = 0.25 * math.sqrt(D) / (student.shape[0] * tok_count)
    teacher_part = jnp.dot(teacher, weight_panel, preferred_element_type=jnp.float32)
    student_part = jnp.dot(student, weight_panel, preferred_element_type=jnp.float32)
    mismatch = reduce_rows((teacher_part - student_part) * scale, "pan")
    first_row = lax.axis_index("tok") * rows
    owned = lax.dynamic_slice_in_dim(weight_panel, first_row, rows, 0).astype(jnp.float32)
    for step in range(ITERS):
        rounded = spread(mismatch.astype(jnp.bfloat16), "pan")
        gradient = lax.dot_general(
            student, rounded, (((0,), (0,)), ((), ())), preferred_element_type=jnp.float32
        )
        change = coef * reduce_rows(gradient, "tok")
        owned = owned + change
        moved = jnp.dot(
            student,
            spread(change.astype(jnp.bfloat16), "tok"),
            preferred_element_type=jnp.float32,
        )
        mismatch = mismatch - reduce_rows(moved * scale, "pan")
    return (owned, spread(mismatch, "pan"))


def solution(mesh):
    in_specs = (P("tok", "pan"), P("tok", "pan"), P("pan", None))
    out_specs = (P(("pan", "tok"), None), P("tok", None))
    return jax.shard_map(local, mesh=mesh, in_specs=in_specs, out_specs=out_specs, check_vma=False)
```

time: 1200 us -> 191 us (0.16)
  waiting for transfers between devices: 914 us -> 15.1 us
  blocking collectives: 253 us -> 157 us
  between operations: 13.8 us -> 0.8 us
    unnamed x7 -> x0, waiting for transfers between devices: 531 us -> none
    psum x3 -> x0, waiting for transfers between devices: 383 us -> none  [the longest x2 299 us: local(): student_sum = lax.psum(partial_proj, 'pan')]
    all_gather x2 -> x0, blocking collectives: 253 us -> none  [local(): lax.all_gather(owned.astype(jnp.bfloat16), 'tok', axis=0, tiled=True)]
    all_to_all x0 -> x9, blocking collectives: none -> 157 us  [exchange(): return lax.all_to_all(blocks, axis, 0, 0, tiled=True)]
    all_to_all x0 -> x1, waiting for transfers between devices: none -> 15.1 us  [exchange(): return lax.all_to_all(blocks, axis, 0, 0, tiled=True)]
  transfers between devices with their start and end apart: 5 -> 1, of which waited for: 5 -> 1; matrix products, arithmetic and copies ran while one was open for 0% -> 0% of each run, Pallas kernels for 0% -> 0%
where the time goes in v1:
time: 191 us; the launch traced here: 190 us
  blocking collectives  157 us (82%)
  waiting for transfers between devices  15.1 us (8%)
  matrix products  6.65 us (3%)
  starting transfers between devices  6.02 us (3%)
  local copies, waits for them, and re-layouts  3.45 us (2%)
    all_to_all x9, blocking collectives, exchange(): return lax.all_to_all(blocks, axis, 0, 0, tiled=True)  157 us
    all_to_all x1, waiting for transfers between devices, exchange(): return lax.all_to_all(blocks, axis, 0, 0, tiled=True)  15.1 us
    all_to_all x1, starting transfers between devices, exchange(): return lax.all_to_all(blocks, axis, 0, 0, tiled=True)  6.02 us
  transfers between devices with their start and end apart: 1, of which 1 were waited for; matrix products, arithmetic and copies ran while one was open for 0% of the time, Pallas kernels for 0%

profile of v1, /device:TPU:1, one launch (start us, length us, event | category | flops | bytes accessed | tf_op | source)
XLA Modules:
  0.0 189.8 jit_solution(16199045186940453393)
XLA Ops:
  0.6 0.0 copy-start
  0.6 0.0 copy-start.1
  0.7 2.5 %fusion.9 = f32[512,128]{1,0:T(8,128)S(1)} fusion(bf16[512,2048]{1,0:T(8,128)(2,1)} %param.4, bf16[2048,128]{1,0:T(8,128)(2,1)} %param.5), kind=kOutput, calls=%fused_computation.22 | convolution fusion | flops 268435456 | bytes 2883584 | tf_op jit(solution)/shard_map/dot_general | solution.py:34
  3.2 0.0 copy-done
  3.2 0.0 copy-done.1
  3.2 0.7 fusion.3
  3.9 20.3 %all_to_all.50 = bf16[8,64,128]{2,1,0:T(8,128)(2,1)S(1)} all-to-all(bf16[8,64,128]{2,1,0:T(8,128)(2,1)S(1)} %bitcast.35), channel_id=1, replica_groups=mesh['tok'=64,'pan'=8] {'pan'}, dimensions={0} | all-to-all | bytes 262144 | tf_op jit(solution)/shard_map/all_to_all | solution.py:13
  24.3 11.7 %all_to_all.51 = bf16[8,64,128]{2,1,0:T(8,128)(2,1)S(1)} all-to-all(bf16[8,64,128]{2,1,0:T(8,128)(2,1)S(1)} %broadcast_in_dim.10), channel_id=1, replica_groups=mesh['tok'=64,'pan'=8] {'pan'}, dimensions={0} | all-to-all | bytes 262144 | tf_op jit(solution)/shard_map/all_to_all | solution.py:13
  36.0 1.3 fusion
  37.3 1.3 copy.5
  38.6 25.4 %all_to_all.52 = bf16[64,32,128]{2,1,0:T(8,128)(2,1)S(1)} all-to-all(bf16[64,32,128]{2,1,0:T(8,128)(2,1)S(1)} %bitcast.31), channel_id=1, replica_groups=mesh['tok'=64,'pan'=8] {'tok'}, dimensions={0} | all-to-all | bytes 1048576 | tf_op jit(solution)/shard_map/all_to_all | solution.py:13
  64.0 0.1 convert_reduce_fusion.1
  64.1 0.1 broadcast_in_dim.11
  64.2 21.9 %all_to_all.53 = bf16[64,32,128]{2,1,0:T(8,128)(2,1)S(1)} all-to-all(bf16[64,32,128]{2,1,0:T(8,128)(2,1)S(1)} %broadcast_in_dim.11), channel_id=1, replica_groups=mesh['tok'=64,'pan'=8] {'tok'}, dimensions={0} | all-to-all | bytes 1048576 | tf_op jit(solution)/shard_map/all_to_all | solution.py:13
  86.1 0.8 fusion.7
  86.9 0.1 copy.6
  87.0 15.6 %all_to_all.54 = bf16[8,64,128]{2,1,0:T(8,128)(2,1)S(1)} all-to-all(bf16[8,64,128]{2,1,0:T(8,128)(2,1)S(1)} %bitcast.36), channel_id=1, replica_groups=mesh['tok'=64,'pan'=8] {'pan'}, dimensions={0} | all-to-all | bytes 262144 | tf_op jit(solution)/shard_map/all_to_all | solution.py:13
  102.7 11.6 %all_to_all.55 = bf16[8,64,128]{2,1,0:T(8,128)(2,1)S(1)} all-to-all(bf16[8,64,128]{2,1,0:T(8,128)(2,1)S(1)} %broadcast_in_dim.12), channel_id=1, replica_groups=mesh['tok'=64,'pan'=8] {'pan'}, dimensions={0} | all-to-all | bytes 262144 | tf_op jit(solution)/shard_map/all_to_all | solution.py:13
  114.3 0.5 fusion.1
  114.8 1.0 copy.7
  115.8 6.0 %all-to-all-start.6 = ((bf16[64,32,128]{2,1,0:T(8,128)(2,1)}), bf16[64,32,128]{2,1,0:T(8,128)(2,1)S(1)}, u32[]{:S(2)}, u32[]{:S(2)}) async-start(bf16[64,32,128]{2,1,0:T(8,128)(2,1)} %bitcast.30), calls=%async_computation.6 | async-start | bytes 1048576 | tf_op jit(solution)/shard_map/all_to_all | solution.py:13
  121.8 15.1 %all-to-all-done.6 = bf16[64,32,128]{2,1,0:T(8,128)(2,1)S(1)} async-done(((bf16[64,32,128]{2,1,0:T(8,128)(2,1)}), bf16[64,32,128]{2,1,0:T(8,128)(2,1)S(1)}, u32[]{:S(2)}, u32[]{:S(2)}) %all-to-all-start.6) | async-done | bytes 524320 | tf_op jit(solution)/shard_map/all_to_all | solution.py:13
  137.0 0.1 convert_reduce_fusion
  137.1 0.6 multiply_convert_fusion
  137.7 0.1 broadcast_in_dim.13
  137.7 22.3 %all_to_all.56 = bf16[64,32,128]{2,1,0:T(8,128)(2,1)S(1)} all-to-all(bf16[64,32,128]{2,1,0:T(8,128)(2,1)S(1)} %broadcast_in_dim.13), channel_id=1, replica_groups=mesh['tok'=64,'pan'=8] {'tok'}, dimensions={0} | all-to-all | bytes 1048576 | tf_op jit(solution)/shard_map/all_to_all | solution.py:13
  160.1 0.8 fusion.6
  160.9 0.1 copy.8
  161.0 14.8 %all_to_all.57 = bf16[8,64,128]{2,1,0:T(8,128)(2,1)S(1)} all-to-all(bf16[8,64,128]{2,1,0:T(8,128)(2,1)S(1)} %bitcast.37), channel_id=1, replica_groups=mesh['tok'=64,'pan'=8] {'pan'}, dimensions={0} | all-to-all | bytes 262144 | tf_op jit(solution)/shard_map/all_to_all | solution.py:13
  175.9 13.2 %all_to_all.58 = f32[8,64,128]{2,1,0:T(8,128)S(1)} all-to-all(f32[8,64,128]{2,1,0:T(8,128)S(1)} %broadcast_in_dim.14), channel_id=1, replica_groups=mesh['tok'=64,'pan'=8] {'pan'}, dimensions={0} | all-to-all | bytes 524288 | tf_op jit(solution)/shard_map/all_to_all | solution.py:13
  189.1 0.7 copy.10
  (10 shorter events, 0.1 us)
Async XLA Ops:
  0.6 2.6 %copy-start = (bf16[512,2048]{1,0:T(8,128)(2,1)S(1)}, bf16[512,2048]{1,0:T(8,128)(2,1)}, u32[]{:S(2)}) copy-start(bf16[512,2048]{1,0:T(8,128)(2,1)} %param.3) | copy-start | bytes 6291460
  0.6 2.6 %copy-start.1 = (bf16[2048,128]{1,0:T(8,128)(2,1)S(1)}, bf16[2048,128]{1,0:T(8,128)(2,1)}, u32[]{:S(2)}) copy-start(bf16[2048,128]{1,0:T(8,128)(2,1)} %param.5) | copy-start | bytes 1572868
  115.8 21.2 %all-to-all-start.6 = ((bf16[64,32,128]{2,1,0:T(8,128)(2,1)}), bf16[64,32,128]{2,1,0:T(8,128)(2,1)S(1)}, u32[]{:S(2)}, u32[]{:S(2)}) async-start(bf16[64,32,128]{2,1,0:T(8,128)(2,1)} %bitcast.30), calls=%async_computation.6 | async-start | bytes 1048576 | tf_op jit(solution)/shard_map/all_to_all | solution.py:13

commit v2 on v1

v2 whole, which is shorter than its diff:
```python
import math

import jax
import jax.numpy as jnp
from jax import lax
from jax.sharding import PartitionSpec as P

D = 16384
ITERS = 2
TOK = ("x", "y_hi", "y_lo", "z_lo")
PAN = ("z_hi", "core")
NEAR = ("x", "y_lo", "z_lo")
FAR = ("y_hi",)


def exchange(blocks, axis):
    return lax.all_to_all(blocks, axis, 0, 0, tiled=True)


def copies(own, axis):
    return exchange(jnp.broadcast_to(own[None], (lax.axis_size(axis),) + own.shape), axis)


def add(blocks):
    return jnp.sum(blocks.astype(jnp.float32), axis=0)


def pan_sum(partial):
    rows = partial.shape[0] // lax.axis_size("core")
    both = lax.all_gather(partial, "core", axis=0, tiled=True)
    first_row = lax.axis_index("core") * rows
    here = lax.dynamic_slice_in_dim(both, first_row, rows, 0)
    there = lax.dynamic_slice_in_dim(both, first_row + partial.shape[0], rows, 0)
    return add(copies((here + there).astype(jnp.bfloat16), "z_hi"))


def tok_sum(partial, factor):
    blocks = partial.astype(jnp.bfloat16).reshape((lax.axis_size(NEAR), -1) + partial.shape[1:])
    near = add(exchange(blocks, NEAR)).astype(jnp.bfloat16)
    total = (factor * add(copies(near, FAR))).astype(jnp.bfloat16)
    return copies(total, NEAR).reshape(partial.shape)


def local(student, teacher, weight_panel):
    tok_count = lax.axis_size(TOK)
    rows = student.shape[1] // tok_count
    scale = 1.0 / math.sqrt(D)
    coef = 0.25 * math.sqrt(D) / (student.shape[0] * tok_count)
    first_row = lax.axis_index(TOK) * rows

    def owned_rows(panel):
        return lax.dynamic_slice_in_dim(panel, first_row, rows, 0).astype(jnp.float32)

    teacher_part = jnp.dot(teacher, weight_panel, preferred_element_type=jnp.float32)
    student_part = jnp.dot(student, weight_panel, preferred_element_type=jnp.float32)
    mismatch = pan_sum((teacher_part - student_part) * scale)
    owned = owned_rows(weight_panel)
    for step in range(ITERS):
        rounded = lax.all_gather(mismatch.astype(jnp.bfloat16), "core", axis=0, tiled=True)
        gradient = lax.dot_general(
            student, rounded, (((0,), (0,)), ((), ())), preferred_element_type=jnp.float32
        )
        change = tok_sum(gradient, coef)
        owned = owned + owned_rows(change)
        moved = jnp.dot(student, change, preferred_element_type=jnp.float32)
        mismatch = mismatch - pan_sum(moved * scale)
    return (owned, lax.all_gather(mismatch, "core", axis=0, tiled=True))


def solution(mesh):
    fine = jax.sharding.Mesh(mesh.devices.reshape(4, 4, 2, 2, 4, 2), TOK + PAN)
    in_specs = (P(TOK, PAN), P(TOK, PAN), P(PAN, None))
    out_specs = (P(PAN + TOK, None), P(TOK, None))
    return jax.shard_map(local, mesh=fine, in_specs=in_specs, out_specs=out_specs, check_vma=False)
```

time: 191 us -> 154 us (0.81)
  blocking collectives: 157 us -> 132 us
  waiting for transfers between devices: 15.1 us -> 7.96 us
  starting transfers between devices: 6.02 us -> 3.41 us
    all_to_all x9 -> x8, blocking collectives: 157 us -> 98 us  [exchange(): return lax.all_to_all(blocks, axis, 0, 0, tiled=True)]
    all_gather x0 -> x6, blocking collectives: none -> 33.5 us  [the longest x3 20.4 us: pan_sum(): both = lax.all_gather(partial, 'core', axis=0, tiled=True)]
    all_to_all x1, waiting for transfers between devices: 15.1 us -> 7.96 us  [exchange(): return lax.all_to_all(blocks, axis, 0, 0, tiled=True)]
    all_to_all x1, starting transfers between devices: 6.02 us -> 3.41 us  [exchange(): return lax.all_to_all(blocks, axis, 0, 0, tiled=True)]
    convert_element_type x4 -> x2, local copies, waits for them, and re-layouts: 2.54 us -> 0.22 us  [pan_sum(): return add(copies((here + there).astype(jnp.bfloat16), 'z_hi'))]
  transfers between devices with their start and end apart: 1 -> 1, of which waited for: 1 -> 1; matrix products, arithmetic and copies ran while one was open for 0% -> 1% of each run, Pallas kernels for 0% -> 0%
where the time goes in v2:
time: 154 us
  blocking collectives  132 us (86%)
  waiting for transfers between devices  7.96 us (5%)
  matrix products  5.84 us (4%)
  starting transfers between devices  3.41 us (2%)
  local copies, waits for them, and re-layouts  2.47 us (2%)
  other arithmetic  1.74 us (1%)
    all_to_all x8, blocking collectives, exchange(): return lax.all_to_all(blocks, axis, 0, 0, tiled=True)  98 us
    all_gather x3, blocking collectives, pan_sum(): both = lax.all_gather(partial, 'core', axis=0, tiled=True)  20.4 us
    all_gather x2, blocking collectives, local(): lax.all_gather(mismatch.astype(jnp.bfloat16), 'core', axis=0, tiled=True)  9.01 us
    all_to_all x1, waiting for transfers between devices, exchange(): return lax.all_to_all(blocks, axis, 0, 0, tiled=True)  7.96 us
    all_gather x1, blocking collectives, local(): return (owned, lax.all_gather(mismatch, 'core', axis=0, tiled=True))  4.1 us
    all_to_all x1, starting transfers between devices, exchange(): return lax.all_to_all(blocks, axis, 0, 0, tiled=True)  3.41 us
  transfers between devices with their start and end apart: 1, of which 1 were waited for; matrix products, arithmetic and copies ran while one was open for 1% of the time, Pallas kernels for 0%

profile of v2, /device:TPU:1, one launch (start us, length us, event | category | flops | bytes accessed | tf_op | source)
XLA Modules:
  0.0 153.8 jit_solution(17306522454890165722)
XLA Ops:
  0.6 0.0 copy-start
  0.6 0.0 copy-start.1
  0.7 2.5 %fusion.6 = f32[512,128]{1,0:T(8,128)S(1)} fusion(bf16[512,2048]{1,0:T(8,128)(2,1)} %param.4, bf16[2048,128]{1,0:T(8,128)(2,1)} %param.5), kind=kOutput, calls=%fused_computation.24 | convolution fusion | flops 268435456 | bytes 2883584 | tf_op jit(solution)/shard_map/dot_general | solution.py:54
  3.2 0.0 copy-done
  3.2 0.0 copy-done.1
  3.2 0.7 fusion.4
  3.9 8.7 %all_gather.18 = f32[1024,128]{1,0:T(8,128)S(1)} all-gather(f32[512,128]{1,0:T(8,128)S(1)} %fusion.4), channel_id=1, replica_groups=mesh['x'=4,'y_hi'=4,'y_lo'=2,'z_lo'=2,'z_hi'=4,'core'=2] {'core'}, dimensions={0}, use_global_device_ids=true | all-gather | bytes 786432 | tf_op jit(solution)/shard_map/all_gather | solution.py:30
  12.7 13.7 %all_to_all.45 = bf16[4,256,128]{2,1,0:T(8,128)(2,1)S(1)} all-to-all(bf16[4,256,128]{2,1,0:T(8,128)(2,1)S(1)} %broadcast_in_dim.14), channel_id=1, replica_groups=mesh['x'=4,'y_hi'=4,'y_lo'=2,'z_lo'=2,'z_hi'=4,'core'=2] {'z_hi'}, dimensions={0} | all-to-all | bytes 524288 | tf_op jit(solution)/shard_map/all_to_all | solution.py:17
  26.4 4.7 %all_gather.19 = bf16[512,128]{1,0:T(8,128)(2,1)S(1)} all-gather(bf16[256,128]{1,0:T(8,128)(2,1)S(1)} %convert_element_type.72), channel_id=1, replica_groups=mesh['x'=4,'y_hi'=4,'y_lo'=2,'z_lo'=2,'z_hi'=4,'core'=2] {'core'}, dimensions={0}, use_global_device_ids=true | all-gather | bytes 196608 | tf_op jit(solution)/shard_map/all_gather | solution.py:59
  31.2 0.5 fusion
  31.7 0.1 copy.30
  31.8 15.0 %all_to_all.46 = bf16[16,128,128]{1,2,0:T(8,128)(2,1)S(1)} all-to-all(bf16[16,128,128]{1,2,0:T(8,128)(2,1)S(1)} %bitcast.34), channel_id=1, replica_groups=mesh['x'=4,'y_hi'=4,'y_lo'=2,'z_lo'=2,'z_hi'=4,'core'=2] {'x','y_lo','z_..., dimensions={0} | all-to-all | bytes 1048576 | tf_op jit(solution)/shard_map/all_to_all | solution.py:17
  46.8 0.1 reduce_sum.70
  46.9 0.1 copy.17
  47.0 13.0 %all_to_all.47 = bf16[4,128,128]{2,1,0:T(8,128)(2,1)S(1)} all-to-all(bf16[4,128,128]{2,1,0:T(8,128)(2,1)S(1)} %broadcast_in_dim.15), channel_id=1, replica_groups=mesh['x'=4,'y_hi'=4,'y_lo'=2,'z_lo'=2,'z_hi'=4,'core'=2] {'y_hi'}, dimensions={0} | all-to-all | bytes 262144 | tf_op jit(solution)/shard_map/all_to_all | solution.py:17
  60.1 0.1 broadcast_in_dim.16
  60.2 11.4 %all_to_all.48 = bf16[16,128,128]{2,1,0:T(8,128)(2,1)S(1)} all-to-all(bf16[16,128,128]{2,1,0:T(8,128)(2,1)S(1)} %broadcast_in_dim.16), channel_id=1, replica_groups=mesh['x'=4,'y_hi'=4,'y_lo'=2,'z_lo'=2,'z_hi'=4,'core'=2] {'x','y_lo','z_..., dimensions={0} | all-to-all | bytes 1048576 | tf_op jit(solution)/shard_map/all_to_all | solution.py:17
  71.6 0.8 fusion.3
  72.4 6.2 %all_gather.20 = f32[1024,128]{0,1:T(8,128)S(1)} all-gather(f32[512,128]{0,1:T(8,128)S(1)} %fusion.3), channel_id=1, replica_groups=mesh['x'=4,'y_hi'=4,'y_lo'=2,'z_lo'=2,'z_hi'=4,'core'=2] {'core'}, dimensions={0}, use_global_device_ids=true | all-gather | bytes 786432 | tf_op jit(solution)/shard_map/all_gather | solution.py:30
  78.6 0.1 copy.18
  78.8 11.7 %all_to_all.49 = bf16[4,256,128]{2,1,0:T(8,128)(2,1)S(1)} all-to-all(bf16[4,256,128]{2,1,0:T(8,128)(2,1)S(1)} %broadcast_in_dim.17), channel_id=1, replica_groups=mesh['x'=4,'y_hi'=4,'y_lo'=2,'z_lo'=2,'z_hi'=4,'core'=2] {'z_hi'}, dimensions={0} | all-to-all | bytes 524288 | tf_op jit(solution)/shard_map/all_to_all | solution.py:17
  90.6 4.3 %all_gather.21 = bf16[512,128]{1,0:T(8,128)(2,1)S(1)} all-gather(bf16[256,128]{1,0:T(8,128)(2,1)S(1)} %get-tuple-element.2), channel_id=1, replica_groups=mesh['x'=4,'y_hi'=4,'y_lo'=2,'z_lo'=2,'z_hi'=4,'core'=2] {'core'}, dimensions={0}, use_global_device_ids=true | all-gather | bytes 196608 | tf_op jit(solution)/shard_map/all_gather | solution.py:59
  94.9 0.5 fusion.1
  95.3 0.1 copy.29
  95.5 12.1 %all_to_all.50 = bf16[16,128,128]{1,2,0:T(8,128)(2,1)S(1)} all-to-all(bf16[16,128,128]{1,2,0:T(8,128)(2,1)S(1)} %bitcast.35), channel_id=1, replica_groups=mesh['x'=4,'y_hi'=4,'y_lo'=2,'z_lo'=2,'z_hi'=4,'core'=2] {'x','y_lo','z_..., dimensions={0} | all-to-all | bytes 1048576 | tf_op jit(solution)/shard_map/all_to_all | solution.py:17
  107.6 0.1 reduce_sum.73
  107.6 0.1 copy.21
  107.8 9.6 %all_to_all.51 = bf16[4,128,128]{2,1,0:T(8,128)(2,1)S(1)} all-to-all(bf16[4,128,128]{2,1,0:T(8,128)(2,1)S(1)} %broadcast_in_dim.18), channel_id=1, replica_groups=mesh['x'=4,'y_hi'=4,'y_lo'=2,'z_lo'=2,'z_hi'=4,'core'=2] {'y_hi'}, dimensions={0} | all-to-all | bytes 262144 | tf_op jit(solution)/shard_map/all_to_all | solution.py:17
  117.5 0.1 broadcast_in_dim.19
  117.6 11.5 %all_to_all.52 = bf16[16,128,128]{2,1,0:T(8,128)(2,1)S(1)} all-to-all(bf16[16,128,128]{2,1,0:T(8,128)(2,1)S(1)} %broadcast_in_dim.19), channel_id=1, replica_groups=mesh['x'=4,'y_hi'=4,'y_lo'=2,'z_lo'=2,'z_hi'=4,'core'=2] {'x','y_lo','z_..., dimensions={0} | all-to-all | bytes 1048576 | tf_op jit(solution)/shard_map/all_to_all | solution.py:17
  129.0 0.8 fusion.2
  129.9 5.5 %all_gather.22 = f32[1024,128]{0,1:T(8,128)S(1)} all-gather(f32[512,128]{0,1:T(8,128)S(1)} %fusion.2), channel_id=1, replica_groups=mesh['x'=4,'y_hi'=4,'y_lo'=2,'z_lo'=2,'z_hi'=4,'core'=2] {'core'}, dimensions={0}, use_global_device_ids=true | all-gather | bytes 786432 | tf_op jit(solution)/shard_map/all_gather | solution.py:30
  135.4 0.1 copy.22
  135.5 0.7 broadcast_in_dim.20
  136.3 3.4 %all-to-all-start.8 = ((bf16[4,256,128]{2,1,0:T(8,128)(2,1)}), bf16[4,256,128]{2,1,0:T(8,128)(2,1)S(1)}, u32[]{:S(2)}, u32[]{:S(2)}) async-start(bf16[4,256,128]{2,1,0:T(8,128)(2,1)} %broadcast_in_dim.20), calls=%async_computation.8 | async-start | bytes 524288 | tf_op jit(solution)/shard_map/all_to_all | solution.py:17
  139.7 1.3 convert_add_fusion
  141.0 8.0 %all-to-all-done.8 = bf16[4,256,128]{2,1,0:T(8,128)(2,1)S(1)} async-done(((bf16[4,256,128]{2,1,0:T(8,128)(2,1)}), bf16[4,256,128]{2,1,0:T(8,128)(2,1)S(1)}, u32[]{:S(2)}, u32[]{:S(2)}) %all-to-all-start.8) | async-done | bytes 262176 | tf_op jit(solution)/shard_map/all_to_all | solution.py:17
  149.0 4.1 %all_gather.23 = f32[512,128]{1,0:T(8,128)S(1)} all-gather(f32[256,128]{1,0:T(8,128)S(1)} %sub.11), channel_id=1, replica_groups=mesh['x'=4,'y_hi'=4,'y_lo'=2,'z_lo'=2,'z_hi'=4,'core'=2] {'core'}, dimensions={0}, use_global_device_ids=true | all-gather | bytes 393216 | tf_op jit(solution)/shard_map/all_gather | solution.py:67
  153.1 0.7 copy.32
  (17 shorter events, 0.4 us)
Async XLA Ops:
  0.6 2.6 %copy-start = (bf16[512,2048]{1,0:T(8,128)(2,1)S(1)}, bf16[512,2048]{1,0:T(8,128)(2,1)}, u32[]{:S(2)}) copy-start(bf16[512,2048]{1,0:T(8,128)(2,1)} %param.3) | copy-start | bytes 6291460
  0.6 2.6 %copy-start.1 = (bf16[2048,128]{1,0:T(8,128)(2,1)S(1)}, bf16[2048,128]{1,0:T(8,128)(2,1)}, u32[]{:S(2)}) copy-start(bf16[2048,128]{1,0:T(8,128)(2,1)} %param.5) | copy-start | bytes 1572868
  136.3 12.7 %all-to-all-start.8 = ((bf16[4,256,128]{2,1,0:T(8,128)(2,1)}), bf16[4,256,128]{2,1,0:T(8,128)(2,1)S(1)}, u32[]{:S(2)}, u32[]{:S(2)}) async-start(bf16[4,256,128]{2,1,0:T(8,128)(2,1)} %broadcast_in_dim.20), calls=%async_computation.8 | async-start | bytes 524288 | tf_op jit(solution)/shard_map/all_to_all | solution.py:17

commit v3 on v2

v3 whole, which is shorter than its diff:
```python
import math

import jax
import jax.numpy as jnp
from jax import lax
from jax.experimental import pallas as pl
from jax.experimental.pallas import tpu as pltpu
from jax.sharding import PartitionSpec as P

D = 16384
ITERS = 2
TOK = ("x", "y_hi", "y_lo", "z_lo")
PAN = ("z_hi", "core")
NEAR = ("x", "y_lo", "z_lo")


def exchange(blocks, axis):
    return lax.all_to_all(blocks, axis, 0, 0, tiled=True)


def copies(own, axis):
    return exchange(jnp.broadcast_to(own[None], (lax.axis_size(axis),) + own.shape), axis)


def add(blocks):
    return jnp.sum(blocks.astype(jnp.float32), axis=0)


def ring_sum(own, axis):
    for pairs in ([[0, 1], [2, 3]], [[1, 2], [3, 0]]):
        both = lax.all_gather(own.astype(jnp.bfloat16), axis, axis=0, tiled=True, axis_index_groups=pairs)
        own = add(both.reshape((2,) + own.shape))
    return own


def hold_kernel(src_ref, out_ref, sem):
    copy = pltpu.make_async_copy(src_ref, out_ref, sem)
    copy.start()
    copy.wait()


def hold(array):
    return pl.pallas_call(
        hold_kernel,
        in_specs=[pl.BlockSpec(memory_space=pl.ANY)],
        out_specs=pl.BlockSpec(memory_space=pltpu.VMEM),
        out_shape=jax.ShapeDtypeStruct(array.shape, array.dtype),
        scratch_shapes=[pltpu.SemaphoreType.DMA],
        compiler_params=pltpu.CompilerParams(vmem_limit_bytes=8 * 1024 * 1024),
        name="hold",
    )(array)


def finish_kernel(core_ref, got_ref, panel_ref, owned_ref, mismatch_ref):
    rows, columns = owned_ref.shape
    tokens = mismatch_ref.shape[0]
    mismatch_ref[...] = got_ref[:, :tokens].T
    last = got_ref[:, tokens:].T
    owned_ref[...] = panel_ref[...] + jnp.where(core_ref[0] == 0, last[:rows], last[rows : 2 * rows])


def finish(core, got, panel_rows, tokens):
    columns = got.shape[0]
    whole = pl.BlockSpec(memory_space=pltpu.VMEM)
    return tuple(
        pl.pallas_call(
            finish_kernel,
            in_specs=[pl.BlockSpec(memory_space=pltpu.SMEM), whole, whole],
            out_specs=[whole, whole],
            out_shape=[
                jax.ShapeDtypeStruct(panel_rows.shape, jnp.float32),
                jax.ShapeDtypeStruct((tokens, columns), jnp.float32),
            ],
            compiler_params=pltpu.CompilerParams(vmem_limit_bytes=8 * 1024 * 1024),
            name="finish",
        )(core, got, panel_rows)
    )


def product(a, b, a_dim, b_dim):
    return lax.dot_general(a, b, (((a_dim,), (b_dim,)), ((), ())), preferred_element_type=jnp.float32)


def split(wide, parts):
    return wide.reshape(wide.shape[0], parts, -1).transpose(1, 0, 2)


def join(blocks):
    return blocks.transpose(1, 0, 2).reshape(blocks.shape[1], -1)


def local(student, teacher, weight_panel):
    tok_count = lax.axis_size(TOK)
    near_count = lax.axis_size(NEAR)
    core = lax.axis_index("core")
    features = student.shape[1]
    tokens = student.shape[0]
    half = weight_panel.shape[1] // 2
    rows = features // tok_count
    scale = 1.0 / math.sqrt(D)
    coef = 0.25 * math.sqrt(D) / (tokens * tok_count)
    first_row = lax.axis_index(TOK) * rows

    student_other = lax.ppermute(student, "core", [(0, 1), (1, 0)])
    student_part = product(weight_panel, student, 0, 1)
    teacher, student_part = lax.optimization_barrier((teacher, student_part))
    partial = (product(weight_panel, teacher, 0, 1) - student_part) * scale
    both = lax.all_gather(partial, "core", axis=0, tiled=True)
    both, student_other = lax.optimization_barrier((both, student_other))
    student_other = hold(student_other)
    here = lax.dynamic_slice_in_dim(both, core * half, half, 0)
    there = lax.dynamic_slice_in_dim(both, core * half + 2 * half, half, 0)
    first, student_other = lax.optimization_barrier(((here + there).astype(jnp.bfloat16), student_other))
    mismatch = add(copies(first, "z_hi"))
    changes = []
    for step in range(ITERS):
        rounded = mismatch.astype(jnp.bfloat16)
        gradient = jnp.concatenate(
            [
                split(product(rounded, part, 1, 0).astype(jnp.bfloat16), near_count // 2)
                for part in (student, student_other)
            ],
            axis=0,
        )
        near = add(exchange(gradient, NEAR))
        change = copies((coef * ring_sum(near, "y_hi")).astype(jnp.bfloat16), NEAR)
        changes.append(change)
        own = join(change[: near_count // 2])
        other = join(change[near_count // 2 :])
        moved = product(own, student, 1, 1) + product(other, student_other, 1, 1)
        if step == ITERS - 1:
            moved, changes, weight_panel = lax.optimization_barrier((moved, changes, weight_panel))
        mismatch = mismatch - add(copies((moved * scale).astype(jnp.bfloat16), "z_hi"))
    width = changes[0].shape[2]
    at = (first_row // width, 0, first_row % width)
    beside = (near_count // 2 + first_row // width, 0, first_row % width)

    def rows_of(start):
        return sum(
            lax.dynamic_slice(change, start, (1, half, rows))[0].astype(jnp.float32) for change in changes
        )

    moved_own, moved_other = rows_of(at), rows_of(beside)
    by_core = jnp.where(
        core == 0,
        jnp.concatenate([moved_own, moved_other], axis=1),
        jnp.concatenate([moved_other, moved_own], axis=1),
    )
    pad = jnp.zeros((half, 128 - 2 * rows), jnp.float32)
    panel_rows = lax.dynamic_slice_in_dim(weight_panel, first_row, rows, 0).astype(jnp.float32)
    got = lax.all_gather(jnp.concatenate([mismatch, by_core, pad], axis=1), "core", axis=0, tiled=True)
    return finish(core.astype(jnp.int32).reshape(1), got, panel_rows, tokens)


def solution(mesh):
    fine = jax.sharding.Mesh(mesh.devices.reshape(4, 4, 2, 2, 4, 2), TOK + PAN)
    in_specs = (P(TOK, PAN), P(TOK, PAN), P(PAN, None))
    out_specs = (P(PAN + TOK, None), P(TOK, None))
    return jax.shard_map(local, mesh=fine, in_specs=in_specs, out_specs=out_specs, check_vma=False)
```

time: 154 us -> 148 us (0.961)
  blocking collectives: 132 us -> 110 us
  starting transfers between devices: 3.41 us -> 12.3 us
  Pallas kernels: 0 us -> 2.59 us
  matrix products: 5.84 us -> 8.4 us
    all_to_all x8 -> x6, blocking collectives: 98 us -> 72.9 us  [exchange(): return lax.all_to_all(blocks, axis, 0, 0, tiled=True)]
    ppermute x0 -> x1, starting transfers between devices: none -> 8.92 us  [local(): student_other = lax.ppermute(student, 'core', [(0, 1), (1, 0)])]
    all_gather x6, blocking collectives: 33.5 us -> 37.6 us  [the longest x4 20.7 us: ring_sum(): lax.all_gather(own.astype(jnp.bfloat16), axis, axis=0, tiled=True, axis_i...]
    pallas_call x0 -> x2, Pallas kernels: none -> 2.59 us  [the longest x1 1.75 us: hold(): pl.pallas_call(hold_kernel, in_specs=[pl.BlockSpec(memory_space=pl.ANY)],...]
    dot_general x6 -> x10, matrix products: 5.84 us -> 8.4 us  [product(): lax.dot_general(a, b, (((a_dim,), (b_dim,)), ((), ())), preferred_element...]
  transfers between devices with their start and end apart: 1 -> 2, of which waited for: 1 -> 1; matrix products, arithmetic and copies ran while one was open for 1% -> 3% of each run, Pallas kernels for 0% -> 0%
where the time goes in v3:
time: 148 us; the launch traced here: 147 us
  blocking collectives  110 us (74%)
  starting transfers between devices  12.3 us (8%)
  matrix products  8.4 us (6%)
  waiting for transfers between devices  7.05 us (5%)
  local copies, waits for them, and re-layouts  3.24 us (2%)
  Pallas kernels  2.59 us (2%)
  other arithmetic  2.07 us (1%)
    all_to_all x6, blocking collectives, exchange(): return lax.all_to_all(blocks, axis, 0, 0, tiled=True)  72.9 us
    all_gather x4, blocking collectives, ring_sum(): lax.all_gather(own.astype(jnp.bfloat16), axis, axis=0, tiled=True, axis_i...  20.7 us
    all_gather x1, blocking collectives, local(): lax.all_gather(jnp.concatenate([mismatch, by_core, pad], axis=1), 'core',...  14.7 us
    ppermute x1, starting transfers between devices, local(): student_other = lax.ppermute(student, 'core', [(0, 1), (1, 0)])  8.92 us
    dot_general x10, matrix products, product(): lax.dot_general(a, b, (((a_dim,), (b_dim,)), ((), ())), preferred_element...  8.4 us
    all_to_all x1, waiting for transfers between devices, exchange(): return lax.all_to_all(blocks, axis, 0, 0, tiled=True)  7.05 us
    all_to_all x1, starting transfers between devices, exchange(): return lax.all_to_all(blocks, axis, 0, 0, tiled=True)  3.41 us
  transfers between devices with their start and end apart: 2, of which 1 were waited for; matrix products, arithmetic and copies ran while one was open for 3% of the time, Pallas kernels for 0%

profile of v3, /device:TPU:1, one launch (start us, length us, event | category | flops | bytes accessed | tf_op | source)
XLA Modules:
  0.0 147.2 jit_solution(5446433501812813559)
XLA Ops:
  0.6 0.0 copy-start
  0.6 0.0 copy-start.7
  0.7 8.9 %collective-permute-start = (bf16[512,2048]{1,0:T(8,128)(2,1)}, bf16[512,2048]{1,0:T(8,128)(2,1)}, u32[]{:S(2)}, u32[]{:S(2)}) collective-permute-start(bf16[512,2048]{1,0:T(8,128)(2,1)} %param.3), channel_id=1, source_target_pairs={{0,1},{1,0},{2,3},{3,2},{4,5},{5,4},{6,7},{7,6},{8,9},{9,8},{10,11... | collective-permute-start | bytes 6291464 | tf_op jit(solution)/shard_map/ppermute | solution.py:104
  9.6 2.6 %fusion.8 = f32[128,512]{1,0:T(8,128)S(1)} fusion(bf16[2048,128]{1,0:T(8,128)(2,1)} %param.5, bf16[512,2048]{1,0:T(8,128)(2,1)} %param.3), kind=kOutput, calls=%fused_computation.39 | convolution fusion | flops 268435456 | bytes 2883584 | tf_op jit(solution)/shard_map/dot_general | solution.py:81
  12.2 0.0 copy-done
  12.2 0.0 copy-done.7
  12.2 0.8 fusion.1
  13.1 2.2 %all_gather.18 = f32[256,512]{1,0:T(8,128)S(1)} all-gather(f32[128,512]{1,0:T(8,128)S(1)} %fusion.1), channel_id=1, replica_groups=mesh['x'=4,'y_hi'=4,'y_lo'=2,'z_lo'=2,'z_hi'=4,'core'=2] {'core'}, dimensions={0}, use_global_device_ids=true | all-gather | bytes 786432 | tf_op jit(solution)/shard_map/all_gather | solution.py:108
  15.2 0.0 copy-start.4
  15.2 0.0 collective-permute-done.src_ref
  15.2 1.7 %hold.1 = bf16[512,2048]{1,0:T(8,128)(2,1)S(1)} custom-call(bf16[512,2048]{1,0:T(8,128)(2,1)} %collective-permute-done.src_ref), custom_call_target="tpu_custom_call" | custom-call | tf_op jit(solution)/shard_map/hold/pallas_call | solution.py:43
  17.0 0.0 copy-start.1
  17.1 13.7 %all_to_all.35 = bf16[4,64,512]{2,1,0:T(8,128)(2,1)S(1)} all-to-all(bf16[4,64,512]{2,1,0:T(8,128)(2,1)S(1)} %broadcast_in_dim.12), channel_id=1, replica_groups=mesh['x'=4,'y_hi'=4,'y_lo'=2,'z_lo'=2,'z_hi'=4,'core'=2] {'z_hi'}, dimensions={0} | all-to-all | bytes 524288 | tf_op jit(solution)/shard_map/all_to_all | solution.py:18
  30.8 0.0 copy-done.4
  30.9 0.5 convolution_convert_fusion.3
  31.3 0.5 convolution_convert_fusion.2
  31.8 0.0 copy-done.1
  32.0 14.6 %all_to_all.36 = bf16[16,64,256]{2,1,0:T(8,128)(2,1)S(1)} all-to-all(bf16[16,64,256]{2,1,0:T(8,128)(2,1)S(1)} %pad_maximum_fusion), channel_id=1, replica_groups=mesh['x'=4,'y_hi'=4,'y_lo'=2,'z_lo'=2,'z_hi'=4,'core'=2] {'x','y_lo','z_..., dimensions={0} | all-to-all | bytes 1048576 | tf_op jit(solution)/shard_map/all_to_all | solution.py:18
  46.6 0.1 reduce_sum.94
  46.7 4.3 %all_gather.19 = bf16[128,256]{1,0:T(8,128)(2,1)S(1)} all-gather(bf16[64,256]{1,0:T(8,128)(2,1)S(1)} %reduce_sum.94), channel_id=1, replica_groups={{0,32},{64,96},{1,33},{65,97},{2,34},{66,98},{3,35},{67,99},{4,36},{68,..., dimensions={0}, use_global_device_ids=true | all-gather | bytes 98304 | tf_op jit(solution)/shard_map/all_gather | solution.py:31
  51.0 0.0 copy-start.5
  51.0 5.7 %all_gather.20 = bf16[128,256]{1,0:T(8,128)(2,1)S(1)} all-gather(bf16[64,256]{1,0:T(8,128)(2,1)S(1)} %reduce_sum.95), channel_id=1, replica_groups={{32,64},{96,0},{33,65},{97,1},{34,66},{98,2},{35,67},{99,3},{36,68},{10..., dimensions={0}, use_global_device_ids=true | all-gather | bytes 98304 | tf_op jit(solution)/shard_map/all_gather | solution.py:31
  56.8 12.4 %all_to_all.37 = bf16[16,64,256]{2,1,0:T(8,128)(2,1)S(1)} all-to-all(bf16[16,64,256]{2,1,0:T(8,128)(2,1)S(1)} %broadcast_in_dim.13), channel_id=1, replica_groups=mesh['x'=4,'y_hi'=4,'y_lo'=2,'z_lo'=2,'z_hi'=4,'core'=2] {'x','y_lo','z_..., dimensions={0} | all-to-all | bytes 1048576 | tf_op jit(solution)/shard_map/all_to_all | solution.py:18
  69.1 0.0 copy-start.2
  69.2 0.0 copy-done.5
  69.2 0.8 fusion.9
  70.0 0.7 copy-done.2
  70.7 0.8 fusion.3
  71.5 11.0 %all_to_all.38 = bf16[4,64,512]{2,1,0:T(8,128)(2,1)S(1)} all-to-all(bf16[4,64,512]{2,1,0:T(8,128)(2,1)S(1)} %broadcast_in_dim.14), channel_id=1, replica_groups=mesh['x'=4,'y_hi'=4,'y_lo'=2,'z_lo'=2,'z_hi'=4,'core'=2] {'z_hi'}, dimensions={0} | all-to-all | bytes 524288 | tf_op jit(solution)/shard_map/all_to_all | solution.py:18
  82.6 0.5 convolution_convert_fusion
  83.1 0.5 convolution_convert_fusion.1
  83.7 10.8 %all_to_all.39 = bf16[16,64,256]{2,1,0:T(8,128)(2,1)S(1)} all-to-all(bf16[16,64,256]{2,1,0:T(8,128)(2,1)S(1)} %pad_maximum_fusion.1), channel_id=1, replica_groups=mesh['x'=4,'y_hi'=4,'y_lo'=2,'z_lo'=2,'z_hi'=4,'core'=2] {'x','y_lo','z_..., dimensions={0} | all-to-all | bytes 1048576 | tf_op jit(solution)/shard_map/all_to_all | solution.py:18
  94.5 0.1 reduce_sum.98
  94.6 5.0 %all_gather.21 = bf16[128,256]{1,0:T(8,128)(2,1)S(1)} all-gather(bf16[64,256]{1,0:T(8,128)(2,1)S(1)} %reduce_sum.98), channel_id=1, replica_groups={{0,32},{64,96},{1,33},{65,97},{2,34},{66,98},{3,35},{67,99},{4,36},{68,..., dimensions={0}, use_global_device_ids=true | all-gather | bytes 98304 | tf_op jit(solution)/shard_map/all_gather | solution.py:31
  99.6 0.0 copy-start.6
  99.6 5.7 %all_gather.22 = bf16[128,256]{1,0:T(8,128)(2,1)S(1)} all-gather(bf16[64,256]{1,0:T(8,128)(2,1)S(1)} %reduce_sum.99), channel_id=1, replica_groups={{32,64},{96,0},{33,65},{97,1},{34,66},{98,2},{35,67},{99,3},{36,68},{10..., dimensions={0}, use_global_device_ids=true | all-gather | bytes 98304 | tf_op jit(solution)/shard_map/all_gather | solution.py:31
  105.3 10.4 %all_to_all.40 = bf16[16,64,256]{2,1,0:T(8,128)(2,1)S(1)} all-to-all(bf16[16,64,256]{2,1,0:T(8,128)(2,1)S(1)} %broadcast_in_dim.15), channel_id=1, replica_groups=mesh['x'=4,'y_hi'=4,'y_lo'=2,'z_lo'=2,'z_hi'=4,'core'=2] {'x','y_lo','z_..., dimensions={0} | all-to-all | bytes 1048576 | tf_op jit(solution)/shard_map/all_to_all | solution.py:18
  115.8 0.0 copy-start.3
  115.8 0.0 copy-done.6
  115.8 0.8 fusion.10
  116.6 0.7 copy-done.3
  117.3 0.8 convolution_add_fusion
  118.1 0.7 broadcast_in_dim.16
  118.8 3.4 %all-to-all-start.6 = ((bf16[4,64,512]{2,1,0:T(8,128)(2,1)}), bf16[4,64,512]{2,1,0:T(8,128)(2,1)S(1)}, u32[]{:S(2)}, u32[]{:S(2)}) async-start(bf16[4,64,512]{2,1,0:T(8,128)(2,1)} %broadcast_in_dim.16), calls=%async_computation.6 | async-start | bytes 524288 | tf_op jit(solution)/shard_map/all_to_all | solution.py:18
  122.3 0.7 pad.2.clone
  123.0 0.7 dynamic-slice_convert_fusion.panel_ref
  123.7 0.1 add_bitcast_fusion.1
  123.8 0.1 maximum_select_fusion
  123.9 7.0 %all-to-all-done.6 = bf16[4,64,512]{2,1,0:T(8,128)(2,1)S(1)} async-done(((bf16[4,64,512]{2,1,0:T(8,128)(2,1)}), bf16[4,64,512]{2,1,0:T(8,128)(2,1)S(1)}, u32[]{:S(2)}, u32[]{:S(2)}) %all-to-all-start.6) | async-done | bytes 262176 | tf_op jit(solution)/shard_map/all_to_all | solution.py:18
  131.0 0.7 maximum_maximum_fusion
  131.7 14.7 %all_gather.23.got_ref = f32[128,640]{1,0:T(8,128)S(1)} all-gather(f32[64,640]{1,0:T(8,128)S(1)} %maximum_maximum_fusion), channel_id=1, replica_groups=mesh['x'=4,'y_hi'=4,'y_lo'=2,'z_lo'=2,'z_hi'=4,'core'=2] {'core'}, dimensions={0}, use_global_device_ids=true | all-gather | bytes 491520 | tf_op jit(solution)/shard_map/all_gather | solution.py:151
  146.4 0.8 finish.1
  (29 shorter events, 0.7 us)
Async XLA Ops:
  0.6 11.6 %copy-start = (bf16[512,2048]{1,0:T(8,128)(2,1)S(1)}, bf16[512,2048]{1,0:T(8,128)(2,1)}, u32[]{:S(2)}) copy-start(bf16[512,2048]{1,0:T(8,128)(2,1)} %param.4) | copy-start | bytes 6291460
  0.6 11.6 %copy-start.7 = (bf16[2048,128]{1,0:T(8,128)(2,1)S(1)}, bf16[2048,128]{1,0:T(8,128)(2,1)}, u32[]{:S(2)}) copy-start(bf16[2048,128]{1,0:T(8,128)(2,1)} %param.5) | copy-start | bytes 1572868
  0.7 14.6 %collective-permute-start = (bf16[512,2048]{1,0:T(8,128)(2,1)}, bf16[512,2048]{1,0:T(8,128)(2,1)}, u32[]{:S(2)}, u32[]{:S(2)}) collective-permute-start(bf16[512,2048]{1,0:T(8,128)(2,1)} %param.3), channel_id=1, source_target_pairs={{0,1},{1,0},{2,3},{3,2},{4,5},{5,4},{6,7},{7,6},{8,9},{9,8},{10,11... | collective-permute-start | bytes 6291464 | tf_op jit(solution)/shard_map/ppermute | solution.py:104
  15.2 15.6 %copy-start.4 = (bf16[512,2048]{1,0:T(8,128)(2,1)S(1)}, bf16[512,2048]{1,0:T(8,128)(2,1)}, u32[]{:S(2)}) copy-start(bf16[512,2048]{1,0:T(8,128)(2,1)} %param.3) | copy-start | bytes 6291460
  17.0 14.8 %copy-start.1 = (bf16[512,2048]{1,0:T(8,128)(2,1)}, bf16[512,2048]{1,0:T(8,128)(2,1)S(1)}, u32[]{:S(2)}) copy-start(bf16[512,2048]{1,0:T(8,128)(2,1)S(1)} %hold.1) | copy-start | bytes 6291460
  51.0 18.2 %copy-start.5 = (bf16[512,2048]{1,0:T(8,128)(2,1)S(1)}, bf16[512,2048]{1,0:T(8,128)(2,1)}, u32[]{:S(2)}) copy-start(bf16[512,2048]{1,0:T(8,128)(2,1)} %param.3) | copy-start | bytes 6291460
  69.1 1.6 %copy-start.2 = (bf16[512,2048]{1,0:T(8,128)(2,1)S(1)}, bf16[512,2048]{1,0:T(8,128)(2,1)}, u32[]{:S(2)}) copy-start(bf16[512,2048]{1,0:T(8,128)(2,1)} %copy-done.1) | copy-start | bytes 6291460
  99.6 16.3 %copy-start.6 = (bf16[512,2048]{1,0:T(8,128)(2,1)S(1)}, bf16[512,2048]{1,0:T(8,128)(2,1)}, u32[]{:S(2)}) copy-start(bf16[512,2048]{1,0:T(8,128)(2,1)} %param.3) | copy-start | bytes 6291460
  115.8 1.6 %copy-start.3 = (bf16[512,2048]{1,0:T(8,128)(2,1)S(1)}, bf16[512,2048]{1,0:T(8,128)(2,1)}, u32[]{:S(2)}) copy-start(bf16[512,2048]{1,0:T(8,128)(2,1)} %copy-done.1) | copy-start | bytes 6291460
  118.8 12.1 %all-to-all-start.6 = ((bf16[4,64,512]{2,1,0:T(8,128)(2,1)}), bf16[4,64,512]{2,1,0:T(8,128)(2,1)S(1)}, u32[]{:S(2)}, u32[]{:S(2)}) async-start(bf16[4,64,512]{2,1,0:T(8,128)(2,1)} %broadcast_in_dim.16), calls=%async_computation.6 | async-start | bytes 524288 | tf_op jit(solution)/shard_map/all_to_all | solution.py:18

commit v4 on v3

--- a/solution.py
+++ b/solution.py
@@ -103,7 +103,6 @@
 
     student_other = lax.ppermute(student, "core", [(0, 1), (1, 0)])
     student_part = product(weight_panel, student, 0, 1)
-    teacher, student_part = lax.optimization_barrier((teacher, student_part))
     partial = (product(weight_panel, teacher, 0, 1) - student_part) * scale
     both = lax.all_gather(partial, "core", axis=0, tiled=True)
     both, student_other = lax.optimization_barrier((both, student_other))

time: 148 us -> 147 us (level)
  no operation moved by 1% of the time
where the time goes in v4:
time: 147 us
  blocking collectives  110 us (75%)
  starting transfers between devices  12.3 us (8%)
  matrix products  7.84 us (5%)
  waiting for transfers between devices  7.06 us (5%)
  local copies, waits for them, and re-layouts  3.24 us (2%)
  Pallas kernels  2.44 us (2%)
  other arithmetic  2.07 us (1%)
    all_to_all x6, blocking collectives, exchange(): return lax.all_to_all(blocks, axis, 0, 0, tiled=True)  72.9 us
    all_gather x4, blocking collectives, ring_sum(): lax.all_gather(own.astype(jnp.bfloat16), axis, axis=0, tiled=True, axis_i...  20.7 us
    all_gather x1, blocking collectives, local(): lax.all_gather(jnp.concatenate([mismatch, by_core, pad], axis=1), 'core',...  14.7 us
    ppermute x1, starting transfers between devices, local(): student_other = lax.ppermute(student, 'core', [(0, 1), (1, 0)])  8.92 us
    dot_general x10, matrix products, product(): lax.dot_general(a, b, (((a_dim,), (b_dim,)), ((), ())), preferred_element...  7.84 us
    all_to_all x1, waiting for transfers between devices, exchange(): return lax.all_to_all(blocks, axis, 0, 0, tiled=True)  7.06 us
    all_to_all x1, starting transfers between devices, exchange(): return lax.all_to_all(blocks, axis, 0, 0, tiled=True)  3.41 us
  transfers between devices with their start and end apart: 2, of which 1 were waited for; matrix products, arithmetic and copies ran while one was open for 3% of the time, Pallas kernels for 0%

profile of v4, /device:TPU:1, one launch (start us, length us, event | category | flops | bytes accessed | tf_op | source)
XLA Modules:
  0.0 146.6 jit_solution(11463885453416727318)
XLA Ops:
  0.6 0.0 copy-start
  0.6 0.0 copy-start.7
  0.7 8.9 %collective-permute-start = (bf16[512,2048]{1,0:T(8,128)(2,1)}, bf16[512,2048]{1,0:T(8,128)(2,1)}, u32[]{:S(2)}, u32[]{:S(2)}) collective-permute-start(bf16[512,2048]{1,0:T(8,128)(2,1)} %param.3), channel_id=1, source_target_pairs={{0,1},{1,0},{2,3},{3,2},{4,5},{5,4},{6,7},{7,6},{8,9},{9,8},{10,11... | collective-permute-start | bytes 6291464 | tf_op jit(solution)/shard_map/ppermute | solution.py:104
  9.6 0.0 copy-done
  9.6 0.0 copy-start.4
  9.6 2.0 %fusion.7 = f32[128,512]{1,0:T(8,128)S(1)} fusion(bf16[2048,128]{1,0:T(8,128)(2,1)} %param.5, bf16[512,2048]{1,0:T(8,128)(2,1)S(1)} %copy-done), kind=kOutput, calls=%fused_computation.38 | convolution fusion | flops 268435456 | bytes 2883584 | tf_op jit(solution)/shard_map/dot_general | solution.py:81
  11.6 0.0 copy-done.7
  11.6 0.0 copy-done.4
  11.7 0.8 fusion
  12.5 2.2 %all_gather.18 = f32[256,512]{1,0:T(8,128)S(1)} all-gather(f32[128,512]{1,0:T(8,128)S(1)} %fusion), channel_id=1, replica_groups=mesh['x'=4,'y_hi'=4,'y_lo'=2,'z_lo'=2,'z_hi'=4,'core'=2] {'core'}, dimensions={0}, use_global_device_ids=true | all-gather | bytes 786432 | tf_op jit(solution)/shard_map/all_gather | solution.py:107
  14.7 0.0 collective-permute-done.src_ref
  14.7 1.6 %hold.1 = bf16[512,2048]{1,0:T(8,128)(2,1)S(1)} custom-call(bf16[512,2048]{1,0:T(8,128)(2,1)} %collective-permute-done.src_ref), custom_call_target="tpu_custom_call" | custom-call | tf_op jit(solution)/shard_map/hold/pallas_call | solution.py:43
  16.3 0.0 copy-start.1
  16.4 13.8 %all_to_all.35 = bf16[4,64,512]{2,1,0:T(8,128)(2,1)S(1)} all-to-all(bf16[4,64,512]{2,1,0:T(8,128)(2,1)S(1)} %broadcast_in_dim.12), channel_id=1, replica_groups=mesh['x'=4,'y_hi'=4,'y_lo'=2,'z_lo'=2,'z_hi'=4,'core'=2] {'z_hi'}, dimensions={0} | all-to-all | bytes 524288 | tf_op jit(solution)/shard_map/all_to_all | solution.py:18
  30.2 0.5 convolution_convert_fusion.3
  30.7 0.5 convolution_convert_fusion.2
  31.2 0.0 copy-done.1
  31.3 14.6 %all_to_all.36 = bf16[16,64,256]{2,1,0:T(8,128)(2,1)S(1)} all-to-all(bf16[16,64,256]{2,1,0:T(8,128)(2,1)S(1)} %pad_maximum_fusion), channel_id=1, replica_groups=mesh['x'=4,'y_hi'=4,'y_lo'=2,'z_lo'=2,'z_hi'=4,'core'=2] {'x','y_lo','z_..., dimensions={0} | all-to-all | bytes 1048576 | tf_op jit(solution)/shard_map/all_to_all | solution.py:18
  45.9 0.1 reduce_sum.94
  46.0 4.3 %all_gather.19 = bf16[128,256]{1,0:T(8,128)(2,1)S(1)} all-gather(bf16[64,256]{1,0:T(8,128)(2,1)S(1)} %reduce_sum.94), channel_id=1, replica_groups={{0,32},{64,96},{1,33},{65,97},{2,34},{66,98},{3,35},{67,99},{4,36},{68,..., dimensions={0}, use_global_device_ids=true | all-gather | bytes 98304 | tf_op jit(solution)/shard_map/all_gather | solution.py:31
  50.3 0.0 copy-start.5
  50.3 5.7 %all_gather.20 = bf16[128,256]{1,0:T(8,128)(2,1)S(1)} all-gather(bf16[64,256]{1,0:T(8,128)(2,1)S(1)} %reduce_sum.95), channel_id=1, replica_groups={{32,64},{96,0},{33,65},{97,1},{34,66},{98,2},{35,67},{99,3},{36,68},{10..., dimensions={0}, use_global_device_ids=true | all-gather | bytes 98304 | tf_op jit(solution)/shard_map/all_gather | solution.py:31
  56.1 12.4 %all_to_all.37 = bf16[16,64,256]{2,1,0:T(8,128)(2,1)S(1)} all-to-all(bf16[16,64,256]{2,1,0:T(8,128)(2,1)S(1)} %broadcast_in_dim.13), channel_id=1, replica_groups=mesh['x'=4,'y_hi'=4,'y_lo'=2,'z_lo'=2,'z_hi'=4,'core'=2] {'x','y_lo','z_..., dimensions={0} | all-to-all | bytes 1048576 | tf_op jit(solution)/shard_map/all_to_all | solution.py:18
  68.4 0.0 copy-start.2
  68.5 0.0 copy-done.5
  68.5 0.8 fusion.8
  69.3 0.7 copy-done.2
  70.0 0.8 fusion.2
  70.8 11.0 %all_to_all.38 = bf16[4,64,512]{2,1,0:T(8,128)(2,1)S(1)} all-to-all(bf16[4,64,512]{2,1,0:T(8,128)(2,1)S(1)} %broadcast_in_dim.14), channel_id=1, replica_groups=mesh['x'=4,'y_hi'=4,'y_lo'=2,'z_lo'=2,'z_hi'=4,'core'=2] {'z_hi'}, dimensions={0} | all-to-all | bytes 524288 | tf_op jit(solution)/shard_map/all_to_all | solution.py:18
  81.9 0.5 convolution_convert_fusion
  82.4 0.5 convolution_convert_fusion.1
  83.0 10.8 %all_to_all.39 = bf16[16,64,256]{2,1,0:T(8,128)(2,1)S(1)} all-to-all(bf16[16,64,256]{2,1,0:T(8,128)(2,1)S(1)} %pad_maximum_fusion.1), channel_id=1, replica_groups=mesh['x'=4,'y_hi'=4,'y_lo'=2,'z_lo'=2,'z_hi'=4,'core'=2] {'x','y_lo','z_..., dimensions={0} | all-to-all | bytes 1048576 | tf_op jit(solution)/shard_map/all_to_all | solution.py:18
  93.8 0.1 reduce_sum.98
  93.9 5.0 %all_gather.21 = bf16[128,256]{1,0:T(8,128)(2,1)S(1)} all-gather(bf16[64,256]{1,0:T(8,128)(2,1)S(1)} %reduce_sum.98), channel_id=1, replica_groups={{0,32},{64,96},{1,33},{65,97},{2,34},{66,98},{3,35},{67,99},{4,36},{68,..., dimensions={0}, use_global_device_ids=true | all-gather | bytes 98304 | tf_op jit(solution)/shard_map/all_gather | solution.py:31
  98.9 0.0 copy-start.6
  98.9 5.7 %all_gather.22 = bf16[128,256]{1,0:T(8,128)(2,1)S(1)} all-gather(bf16[64,256]{1,0:T(8,128)(2,1)S(1)} %reduce_sum.99), channel_id=1, replica_groups={{32,64},{96,0},{33,65},{97,1},{34,66},{98,2},{35,67},{99,3},{36,68},{10..., dimensions={0}, use_global_device_ids=true | all-gather | bytes 98304 | tf_op jit(solution)/shard_map/all_gather | solution.py:31
  104.6 10.4 %all_to_all.40 = bf16[16,64,256]{2,1,0:T(8,128)(2,1)S(1)} all-to-all(bf16[16,64,256]{2,1,0:T(8,128)(2,1)S(1)} %broadcast_in_dim.15), channel_id=1, replica_groups=mesh['x'=4,'y_hi'=4,'y_lo'=2,'z_lo'=2,'z_hi'=4,'core'=2] {'x','y_lo','z_..., dimensions={0} | all-to-all | bytes 1048576 | tf_op jit(solution)/shard_map/all_to_all | solution.py:18
  115.1 0.0 copy-start.3
  115.1 0.0 copy-done.6
  115.1 0.8 fusion.9
  115.9 0.7 copy-done.3
  116.6 0.8 convolution_add_fusion
  117.4 0.7 broadcast_in_dim.16
  118.1 3.4 %all-to-all-start.6 = ((bf16[4,64,512]{2,1,0:T(8,128)(2,1)}), bf16[4,64,512]{2,1,0:T(8,128)(2,1)S(1)}, u32[]{:S(2)}, u32[]{:S(2)}) async-start(bf16[4,64,512]{2,1,0:T(8,128)(2,1)} %broadcast_in_dim.16), calls=%async_computation.6 | async-start | bytes 524288 | tf_op jit(solution)/shard_map/all_to_all | solution.py:18
  121.6 0.7 pad.2.clone
  122.3 0.7 dynamic-slice_convert_fusion.panel_ref
  123.0 0.1 add_bitcast_fusion.1
  123.1 0.1 maximum_select_fusion
  123.2 7.1 %all-to-all-done.6 = bf16[4,64,512]{2,1,0:T(8,128)(2,1)S(1)} async-done(((bf16[4,64,512]{2,1,0:T(8,128)(2,1)}), bf16[4,64,512]{2,1,0:T(8,128)(2,1)S(1)}, u32[]{:S(2)}, u32[]{:S(2)}) %all-to-all-start.6) | async-done | bytes 262176 | tf_op jit(solution)/shard_map/all_to_all | solution.py:18
  130.3 0.7 maximum_maximum_fusion
  131.0 14.7 %all_gather.23.got_ref = f32[128,640]{1,0:T(8,128)S(1)} all-gather(f32[64,640]{1,0:T(8,128)S(1)} %maximum_maximum_fusion), channel_id=1, replica_groups=mesh['x'=4,'y_hi'=4,'y_lo'=2,'z_lo'=2,'z_hi'=4,'core'=2] {'core'}, dimensions={0}, use_global_device_ids=true | all-gather | bytes 491520 | tf_op jit(solution)/shard_map/all_gather | solution.py:150
  145.7 0.8 finish.1
  (29 shorter events, 0.7 us)
Async XLA Ops:
  0.6 9.0 %copy-start = (bf16[512,2048]{1,0:T(8,128)(2,1)S(1)}, bf16[512,2048]{1,0:T(8,128)(2,1)}, u32[]{:S(2)}) copy-start(bf16[512,2048]{1,0:T(8,128)(2,1)} %param.4) | copy-start | bytes 6291460
  0.6 11.0 %copy-start.7 = (bf16[2048,128]{1,0:T(8,128)(2,1)S(1)}, bf16[2048,128]{1,0:T(8,128)(2,1)}, u32[]{:S(2)}) copy-start(bf16[2048,128]{1,0:T(8,128)(2,1)} %param.5) | copy-start | bytes 1572868
  0.7 14.0 %collective-permute-start = (bf16[512,2048]{1,0:T(8,128)(2,1)}, bf16[512,2048]{1,0:T(8,128)(2,1)}, u32[]{:S(2)}, u32[]{:S(2)}) collective-permute-start(bf16[512,2048]{1,0:T(8,128)(2,1)} %param.3), channel_id=1, source_target_pairs={{0,1},{1,0},{2,3},{3,2},{4,5},{5,4},{6,7},{7,6},{8,9},{9,8},{10,11... | collective-permute-start | bytes 6291464 | tf_op jit(solution)/shard_map/ppermute | solution.py:104
  9.6 2.0 %copy-start.4 = (bf16[512,2048]{1,0:T(8,128)(2,1)S(1)}, bf16[512,2048]{1,0:T(8,128)(2,1)}, u32[]{:S(2)}) copy-start(bf16[512,2048]{1,0:T(8,128)(2,1)} %param.3) | copy-start | bytes 6291460
  16.3 14.9 %copy-start.1 = (bf16[512,2048]{1,0:T(8,128)(2,1)}, bf16[512,2048]{1,0:T(8,128)(2,1)S(1)}, u32[]{:S(2)}) copy-start(bf16[512,2048]{1,0:T(8,128)(2,1)S(1)} %hold.1) | copy-start | bytes 6291460
  50.3 18.2 %copy-start.5 = (bf16[512,2048]{1,0:T(8,128)(2,1)S(1)}, bf16[512,2048]{1,0:T(8,128)(2,1)}, u32[]{:S(2)}) copy-start(bf16[512,2048]{1,0:T(8,128)(2,1)} %param.3) | copy-start | bytes 6291460
  68.4 1.6 %copy-start.2 = (bf16[512,2048]{1,0:T(8,128)(2,1)S(1)}, bf16[512,2048]{1,0:T(8,128)(2,1)}, u32[]{:S(2)}) copy-start(bf16[512,2048]{1,0:T(8,128)(2,1)} %copy-done.1) | copy-start | bytes 6291460
  98.9 16.3 %copy-start.6 = (bf16[512,2048]{1,0:T(8,128)(2,1)S(1)}, bf16[512,2048]{1,0:T(8,128)(2,1)}, u32[]{:S(2)}) copy-start(bf16[512,2048]{1,0:T(8,128)(2,1)} %param.3) | copy-start | bytes 6291460
  115.1 1.6 %copy-start.3 = (bf16[512,2048]{1,0:T(8,128)(2,1)S(1)}, bf16[512,2048]{1,0:T(8,128)(2,1)}, u32[]{:S(2)}) copy-start(bf16[512,2048]{1,0:T(8,128)(2,1)} %copy-done.1) | copy-start | bytes 6291460
  118.1 12.1 %all-to-all-start.6 = ((bf16[4,64,512]{2,1,0:T(8,128)(2,1)}), bf16[4,64,512]{2,1,0:T(8,128)(2,1)S(1)}, u32[]{:S(2)}, u32[]{:S(2)}) async-start(bf16[4,64,512]{2,1,0:T(8,128)(2,1)} %broadcast_in_dim.16), calls=%async_computation.6 | async-start | bytes 524288 | tf_op jit(solution)/shard_map/all_to_all | solution.py:18

commit v5 on v4

--- a/solution.py
+++ b/solution.py
@@ -77,6 +77,28 @@
     )
 
 
+def join_kernel(got_ref, mismatch_ref, by_core_ref, out_ref):
+    tokens = mismatch_ref.shape[1]
+    total = got_ref[0].astype(jnp.float32)
+    for at in range(1, got_ref.shape[0]):
+        total += got_ref[at].astype(jnp.float32)
+    out_ref[:, :tokens] = mismatch_ref[...] - total
+    out_ref[:, tokens:] = by_core_ref[...]
+
+
+def last_joined(got, mismatch, by_core):
+    whole = pl.BlockSpec(memory_space=pltpu.VMEM)
+    shape = (mismatch.shape[0], mismatch.shape[1] + by_core.shape[1])
+    return pl.pallas_call(
+        join_kernel,
+        in_specs=[whole] * 3,
+        out_specs=whole,
+        out_shape=jax.ShapeDtypeStruct(shape, jnp.float32),
+        compiler_params=pltpu.CompilerParams(vmem_limit_bytes=8 * 1024 * 1024),
+        name="last_joined",
+    )(got, mismatch, by_core)
+
+
 def product(a, b, a_dim, b_dim):
     return lax.dot_general(a, b, (((a_dim,), (b_dim,)), ((), ())), preferred_element_type=jnp.float32)
 
@@ -110,7 +132,7 @@
     here = lax.dynamic_slice_in_dim(both, core * half, half, 0)
     there = lax.dynamic_slice_in_dim(both, core * half + 2 * half, half, 0)
     first, student_other = lax.optimization_barrier(((here + there).astype(jnp.bfloat16), student_other))
-    mismatch = add(copies(first, "z_hi"))
+    mismatch = ring_sum(first, "z_hi")
     changes = []
     for step in range(ITERS):
         rounded = mismatch.astype(jnp.bfloat16)
@@ -129,7 +151,9 @@
         moved = product(own, student, 1, 1) + product(other, student_other, 1, 1)
         if step == ITERS - 1:
             moved, changes, weight_panel = lax.optimization_barrier((moved, changes, weight_panel))
-        mismatch = mismatch - add(copies((moved * scale).astype(jnp.bfloat16), "z_hi"))
+        came = copies((moved * scale).astype(jnp.bfloat16), "z_hi")
+        if step < ITERS - 1:
+            mismatch = mismatch - add(came)
     width = changes[0].shape[2]
     at = (first_row // width, 0, first_row % width)
     beside = (near_count // 2 + first_row // width, 0, first_row % width)
@@ -147,7 +171,7 @@
     )
     pad = jnp.zeros((half, 128 - 2 * rows), jnp.float32)
     panel_rows = lax.dynamic_slice_in_dim(weight_panel, first_row, rows, 0).astype(jnp.float32)
-    got = lax.all_gather(jnp.concatenate([mismatch, by_core, pad], axis=1), "core", axis=0, tiled=True)
+    got = lax.all_gather(last_joined(came, mismatch, jnp.concatenate([by_core, pad], axis=1)), "core", axis=0, tiled=True)
     return finish(core.astype(jnp.int32).reshape(1), got, panel_rows, tokens)
 
 

time: 147 us -> 150 us (1.020)
  matrix products: 7.84 us -> 9.46 us
    all_gather x4 -> x6, blocking collectives: 20.7 us -> 31.7 us  [ring_sum(): lax.all_gather(own.astype(jnp.bfloat16), axis, axis=0, tiled=True, axis_i...]
    all_to_all x6 -> x5, blocking collectives: 72.9 us -> 62.9 us  [exchange(): return lax.all_to_all(blocks, axis, 0, 0, tiled=True)]
    dot_general x10, matrix products: 7.84 us -> 9.46 us  [product(): lax.dot_general(a, b, (((a_dim,), (b_dim,)), ((), ())), preferred_element...]
where the time goes in v5:
time: 150 us; the launch traced here: 149 us
  blocking collectives  111 us (74%)
  starting transfers between devices  12.3 us (8%)
  matrix products  9.46 us (6%)
  waiting for transfers between devices  7.27 us (5%)
  local copies, waits for them, and re-layouts  3.89 us (3%)
  Pallas kernels  2.48 us (2%)
    all_to_all x5, blocking collectives, exchange(): return lax.all_to_all(blocks, axis, 0, 0, tiled=True)  62.9 us
    all_gather x6, blocking collectives, ring_sum(): lax.all_gather(own.astype(jnp.bfloat16), axis, axis=0, tiled=True, axis_i...  31.7 us
    all_gather x1, blocking collectives, local(): lax.all_gather(last_joined(came, mismatch, jnp.concatenate([by_core, pad]...  14.7 us
    dot_general x10, matrix products, product(): lax.dot_general(a, b, (((a_dim,), (b_dim,)), ((), ())), preferred_element...  9.46 us
    ppermute x1, starting transfers between devices, local(): student_other = lax.ppermute(student, 'core', [(0, 1), (1, 0)])  8.92 us
    all_to_all x1, waiting for transfers between devices, exchange(): return lax.all_to_all(blocks, axis, 0, 0, tiled=True)  7.26 us
    all_to_all x1, starting transfers between devices, exchange(): return lax.all_to_all(blocks, axis, 0, 0, tiled=True)  3.41 us
  transfers between devices with their start and end apart: 2, of which 1 were waited for; matrix products, arithmetic and copies ran while one was open for 3% of the time, Pallas kernels for 0%

profile of v5, /device:TPU:1, one launch (start us, length us, event | category | flops | bytes accessed | tf_op | source)
XLA Modules:
  0.0 149.2 jit_solution(12891759391222908600)
XLA Ops:
  0.6 0.0 copy-start
  0.6 0.0 copy-start.8
  0.7 8.9 %collective-permute-start = (bf16[512,2048]{1,0:T(8,128)(2,1)}, bf16[512,2048]{1,0:T(8,128)(2,1)}, u32[]{:S(2)}, u32[]{:S(2)}) collective-permute-start(bf16[512,2048]{1,0:T(8,128)(2,1)} %param.3), channel_id=1, source_target_pairs={{0,1},{1,0},{2,3},{3,2},{4,5},{5,4},{6,7},{7,6},{8,9},{9,8},{10,11... | collective-permute-start | bytes 6291464 | tf_op jit(solution)/shard_map/ppermute | solution.py:126
  9.6 0.0 copy-done
  9.6 0.0 copy-start.5
  9.6 2.0 %fusion.7 = f32[128,512]{1,0:T(8,128)S(1)} fusion(bf16[2048,128]{1,0:T(8,128)(2,1)} %param.5, bf16[512,2048]{1,0:T(8,128)(2,1)S(1)} %copy-done), kind=kOutput, calls=%fused_computation.36 | convolution fusion | flops 268435456 | bytes 2883584 | tf_op jit(solution)/shard_map/dot_general | solution.py:103
  11.6 0.0 copy-done.8
  11.6 0.0 copy-done.5
  11.7 0.8 fusion
  12.5 2.2 %all_gather.24 = f32[256,512]{1,0:T(8,128)S(1)} all-gather(f32[128,512]{1,0:T(8,128)S(1)} %fusion), channel_id=1, replica_groups=mesh['x'=4,'y_hi'=4,'y_lo'=2,'z_lo'=2,'z_hi'=4,'core'=2] {'core'}, dimensions={0}, use_global_device_ids=true | all-gather | bytes 786432 | tf_op jit(solution)/shard_map/all_gather | solution.py:129
  14.7 0.0 collective-permute-done.src_ref
  14.7 1.6 %hold.1 = bf16[512,2048]{1,0:T(8,128)(2,1)S(1)} custom-call(bf16[512,2048]{1,0:T(8,128)(2,1)} %collective-permute-done.src_ref), custom_call_target="tpu_custom_call" | custom-call | tf_op jit(solution)/shard_map/hold/pallas_call | solution.py:43
  16.3 0.0 copy-start.1
  16.3 1.3 copy-done.1
  17.7 5.1 %all_gather.25 = bf16[128,512]{1,0:T(8,128)(2,1)S(1)} all-gather(bf16[64,512]{1,0:T(8,128)(2,1)S(1)} %add_convert_fusion), channel_id=1, replica_groups={{0,2},{4,6},{1,3},{5,7},{8,10},{12,14},{9,11},{13,15},{16,18},{20,22},{..., dimensions={0}, use_global_device_ids=true | all-gather | bytes 196608 | tf_op jit(solution)/shard_map/all_gather | solution.py:31
  22.8 0.0 copy-start.2
  22.8 6.0 %all_gather.26 = bf16[128,512]{1,0:T(8,128)(2,1)S(1)} all-gather(bf16[64,512]{1,0:T(8,128)(2,1)S(1)} %reduce_sum.96), channel_id=1, replica_groups={{2,4},{6,0},{3,5},{7,1},{10,12},{14,8},{11,13},{15,9},{18,20},{22,16},{..., dimensions={0}, use_global_device_ids=true | all-gather | bytes 196608 | tf_op jit(solution)/shard_map/all_gather | solution.py:31
  28.9 2.1 %convolution_convert_fusion.3 = bf16[64,2048]{1,0:T(8,128)(2,1)S(1)} fusion(bf16[512,2048]{1,0:T(8,128)(2,1)} %param.3, f32[64,512]{1,0:T(8,128)S(1)} %convert_reduce_fusion.1), kind=kOutput, calls=%fused_computation.3 | convolution fusion | flops 134381568 | bytes 2490368 | tf_op jit(solution)/shard_map/dot_general | solution.py:103
  31.0 0.0 copy-done.2
  31.0 0.5 convolution_convert_fusion.2
  31.6 16.8 %all_to_all.30 = bf16[16,64,256]{2,1,0:T(8,128)(2,1)S(1)} all-to-all(bf16[16,64,256]{2,1,0:T(8,128)(2,1)S(1)} %pad_maximum_fusion), channel_id=1, replica_groups=mesh['x'=4,'y_hi'=4,'y_lo'=2,'z_lo'=2,'z_hi'=4,'core'=2] {'x','y_lo','z_..., dimensions={0} | all-to-all | bytes 1048576 | tf_op jit(solution)/shard_map/all_to_all | solution.py:18
  48.4 0.1 reduce_sum.98
  48.5 4.3 %all_gather.27 = bf16[128,256]{1,0:T(8,128)(2,1)S(1)} all-gather(bf16[64,256]{1,0:T(8,128)(2,1)S(1)} %reduce_sum.98), channel_id=1, replica_groups={{0,32},{64,96},{1,33},{65,97},{2,34},{66,98},{3,35},{67,99},{4,36},{68,..., dimensions={0}, use_global_device_ids=true | all-gather | bytes 98304 | tf_op jit(solution)/shard_map/all_gather | solution.py:31
  52.8 0.0 copy-start.6
  52.8 5.7 %all_gather.28 = bf16[128,256]{1,0:T(8,128)(2,1)S(1)} all-gather(bf16[64,256]{1,0:T(8,128)(2,1)S(1)} %reduce_sum.99), channel_id=1, replica_groups={{32,64},{96,0},{33,65},{97,1},{34,66},{98,2},{35,67},{99,3},{36,68},{10..., dimensions={0}, use_global_device_ids=true | all-gather | bytes 98304 | tf_op jit(solution)/shard_map/all_gather | solution.py:31
  58.6 12.2 %all_to_all.31 = bf16[16,64,256]{2,1,0:T(8,128)(2,1)S(1)} all-to-all(bf16[16,64,256]{2,1,0:T(8,128)(2,1)S(1)} %broadcast_in_dim.8), channel_id=1, replica_groups=mesh['x'=4,'y_hi'=4,'y_lo'=2,'z_lo'=2,'z_hi'=4,'core'=2] {'x','y_lo','z_..., dimensions={0} | all-to-all | bytes 1048576 | tf_op jit(solution)/shard_map/all_to_all | solution.py:18
  70.8 0.0 copy-start.3
  70.9 0.0 copy-done.6
  70.9 0.8 fusion.8
  71.7 0.7 copy-done.3
  72.4 0.8 fusion.2
  73.2 12.5 %all_to_all.32 = bf16[4,64,512]{2,1,0:T(8,128)(2,1)S(1)} all-to-all(bf16[4,64,512]{2,1,0:T(8,128)(2,1)S(1)} %broadcast_in_dim.9), channel_id=1, replica_groups=mesh['x'=4,'y_hi'=4,'y_lo'=2,'z_lo'=2,'z_hi'=4,'core'=2] {'z_hi'}, dimensions={0} | all-to-all | bytes 524288 | tf_op jit(solution)/shard_map/all_to_all | solution.py:18
  85.8 0.5 convolution_convert_fusion
  86.3 0.5 convolution_convert_fusion.1
  86.9 10.8 %all_to_all.33 = bf16[16,64,256]{2,1,0:T(8,128)(2,1)S(1)} all-to-all(bf16[16,64,256]{2,1,0:T(8,128)(2,1)S(1)} %pad_maximum_fusion.1), channel_id=1, replica_groups=mesh['x'=4,'y_hi'=4,'y_lo'=2,'z_lo'=2,'z_hi'=4,'core'=2] {'x','y_lo','z_..., dimensions={0} | all-to-all | bytes 1048576 | tf_op jit(solution)/shard_map/all_to_all | solution.py:18
  97.7 0.1 reduce_sum.102
  97.8 4.8 %all_gather.29 = bf16[128,256]{1,0:T(8,128)(2,1)S(1)} all-gather(bf16[64,256]{1,0:T(8,128)(2,1)S(1)} %reduce_sum.102), channel_id=1, replica_groups={{0,32},{64,96},{1,33},{65,97},{2,34},{66,98},{3,35},{67,99},{4,36},{68,..., dimensions={0}, use_global_device_ids=true | all-gather | bytes 98304 | tf_op jit(solution)/shard_map/all_gather | solution.py:31
  102.6 0.0 copy-start.7
  102.6 5.7 %all_gather.30 = bf16[128,256]{1,0:T(8,128)(2,1)S(1)} all-gather(bf16[64,256]{1,0:T(8,128)(2,1)S(1)} %reduce_sum.103), channel_id=1, replica_groups={{32,64},{96,0},{33,65},{97,1},{34,66},{98,2},{35,67},{99,3},{36,68},{10..., dimensions={0}, use_global_device_ids=true | all-gather | bytes 98304 | tf_op jit(solution)/shard_map/all_gather | solution.py:31
  108.4 10.6 %all_to_all.34 = bf16[16,64,256]{2,1,0:T(8,128)(2,1)S(1)} all-to-all(bf16[16,64,256]{2,1,0:T(8,128)(2,1)S(1)} %broadcast_in_dim.10), channel_id=1, replica_groups=mesh['x'=4,'y_hi'=4,'y_lo'=2,'z_lo'=2,'z_hi'=4,'core'=2] {'x','y_lo','z_..., dimensions={0} | all-to-all | bytes 1048576 | tf_op jit(solution)/shard_map/all_to_all | solution.py:18
  118.9 0.0 copy-start.4
  119.0 0.0 copy-done.7
  119.0 0.8 fusion.9
  119.8 0.7 copy-done.4
  120.5 0.8 convolution_add_fusion
  121.3 0.7 broadcast_in_dim.11
  122.0 3.4 %all-to-all-start.5 = ((bf16[4,64,512]{2,1,0:T(8,128)(2,1)}), bf16[4,64,512]{2,1,0:T(8,128)(2,1)S(1)}, u32[]{:S(2)}, u32[]{:S(2)}) async-start(bf16[4,64,512]{2,1,0:T(8,128)(2,1)} %broadcast_in_dim.11), calls=%async_computation.5 | async-start | bytes 524288 | tf_op jit(solution)/shard_map/all_to_all | solution.py:18
  125.5 0.1 add_bitcast_fusion.1
  125.6 0.1 maximum_select_fusion
  125.7 0.7 dynamic-slice_convert_fusion.panel_ref
  126.4 7.3 %all-to-all-done.5.got_ref = bf16[4,64,512]{2,1,0:T(8,128)(2,1)S(1)} async-done(((bf16[4,64,512]{2,1,0:T(8,128)(2,1)}), bf16[4,64,512]{2,1,0:T(8,128)(2,1)S(1)}, u32[]{:S(2)}, u32[]{:S(2)}) %all-to-all-start.5) | async-done | bytes 262176 | tf_op jit(solution)/shard_map/all_to_all | solution.py:18
  133.7 14.7 %all_gather.31.got_ref = f32[128,640]{1,0:T(8,128)S(1)} all-gather(f32[64,640]{1,0:T(8,128)S(1)} %last_joined.1), channel_id=1, replica_groups=mesh['x'=4,'y_hi'=4,'y_lo'=2,'z_lo'=2,'z_hi'=4,'core'=2] {'core'}, dimensions={0}, use_global_device_ids=true | all-gather | bytes 491520 | tf_op jit(solution)/shard_map/all_gather | solution.py:174
  148.4 0.8 finish.1
  (28 shorter events, 0.7 us)
Async XLA Ops:
  0.6 9.0 %copy-start = (bf16[512,2048]{1,0:T(8,128)(2,1)S(1)}, bf16[512,2048]{1,0:T(8,128)(2,1)}, u32[]{:S(2)}) copy-start(bf16[512,2048]{1,0:T(8,128)(2,1)} %param.4) | copy-start | bytes 6291460
  0.6 11.0 %copy-start.8 = (bf16[2048,128]{1,0:T(8,128)(2,1)S(1)}, bf16[2048,128]{1,0:T(8,128)(2,1)}, u32[]{:S(2)}) copy-start(bf16[2048,128]{1,0:T(8,128)(2,1)} %param.5) | copy-start | bytes 1572868
  0.7 14.0 %collective-permute-start = (bf16[512,2048]{1,0:T(8,128)(2,1)}, bf16[512,2048]{1,0:T(8,128)(2,1)}, u32[]{:S(2)}, u32[]{:S(2)}) collective-permute-start(bf16[512,2048]{1,0:T(8,128)(2,1)} %param.3), channel_id=1, source_target_pairs={{0,1},{1,0},{2,3},{3,2},{4,5},{5,4},{6,7},{7,6},{8,9},{9,8},{10,11... | collective-permute-start | bytes 6291464 | tf_op jit(solution)/shard_map/ppermute | solution.py:126
  9.6 2.0 %copy-start.5 = (bf16[512,2048]{1,0:T(8,128)(2,1)S(1)}, bf16[512,2048]{1,0:T(8,128)(2,1)}, u32[]{:S(2)}) copy-start(bf16[512,2048]{1,0:T(8,128)(2,1)} %param.3) | copy-start | bytes 6291460
  16.3 1.4 copy-start.1
  22.8 8.1 %copy-start.2 = (bf16[512,2048]{1,0:T(8,128)(2,1)S(1)}, bf16[512,2048]{1,0:T(8,128)(2,1)}, u32[]{:S(2)}) copy-start(bf16[512,2048]{1,0:T(8,128)(2,1)} %copy-done.1) | copy-start | bytes 6291460
  52.8 18.1 %copy-start.6 = (bf16[512,2048]{1,0:T(8,128)(2,1)S(1)}, bf16[512,2048]{1,0:T(8,128)(2,1)}, u32[]{:S(2)}) copy-start(bf16[512,2048]{1,0:T(8,128)(2,1)} %param.3) | copy-start | bytes 6291460
  70.8 1.6 %copy-start.3 = (bf16[512,2048]{1,0:T(8,128)(2,1)S(1)}, bf16[512,2048]{1,0:T(8,128)(2,1)}, u32[]{:S(2)}) copy-start(bf16[512,2048]{1,0:T(8,128)(2,1)} %copy-done.1) | copy-start | bytes 6291460
  102.6 16.4 %copy-start.7 = (bf16[512,2048]{1,0:T(8,128)(2,1)S(1)}, bf16[512,2048]{1,0:T(8,128)(2,1)}, u32[]{:S(2)}) copy-start(bf16[512,2048]{1,0:T(8,128)(2,1)} %param.3) | copy-start | bytes 6291460
  118.9 1.6 %copy-start.4 = (bf16[512,2048]{1,0:T(8,128)(2,1)S(1)}, bf16[512,2048]{1,0:T(8,128)(2,1)}, u32[]{:S(2)}) copy-start(bf16[512,2048]{1,0:T(8,128)(2,1)} %copy-done.1) | copy-start | bytes 6291460
  122.0 11.6 %all-to-all-start.5 = ((bf16[4,64,512]{2,1,0:T(8,128)(2,1)}), bf16[4,64,512]{2,1,0:T(8,128)(2,1)S(1)}, u32[]{:S(2)}, u32[]{:S(2)}) async-start(bf16[4,64,512]{2,1,0:T(8,128)(2,1)} %broadcast_in_dim.11), calls=%async_computation.5 | async-start | bytes 524288 | tf_op jit(solution)/shard_map/all_to_all | solution.py:18

commit v6 on v5

--- a/solution.py
+++ b/solution.py
@@ -132,7 +132,7 @@
     here = lax.dynamic_slice_in_dim(both, core * half, half, 0)
     there = lax.dynamic_slice_in_dim(both, core * half + 2 * half, half, 0)
     first, student_other = lax.optimization_barrier(((here + there).astype(jnp.bfloat16), student_other))
-    mismatch = ring_sum(first, "z_hi")
+    mismatch = add(copies(first, "z_hi"))
     changes = []
     for step in range(ITERS):
         rounded = mismatch.astype(jnp.bfloat16)

time: 150 us -> 147 us (0.980)
  matrix products: 9.46 us -> 7.84 us
    all_gather x6 -> x4, blocking collectives: 31.7 us -> 20.7 us  [ring_sum(): lax.all_gather(own.astype(jnp.bfloat16), axis, axis=0, tiled=True, axis_i...]
    all_to_all x5 -> x6, blocking collectives: 62.9 us -> 72.9 us  [exchange(): return lax.all_to_all(blocks, axis, 0, 0, tiled=True)]
    dot_general x10, matrix products: 9.46 us -> 7.84 us  [product(): lax.dot_general(a, b, (((a_dim,), (b_dim,)), ((), ())), preferred_element...]
where the time goes in v6:
time: 147 us; the launch traced here: 146 us
  blocking collectives  110 us (75%)
  starting transfers between devices  12.3 us (8%)
  matrix products  7.84 us (5%)
  waiting for transfers between devices  7.72 us (5%)
  local copies, waits for them, and re-layouts  2.58 us (2%)
  Pallas kernels  2.48 us (2%)
    all_to_all x6, blocking collectives, exchange(): return lax.all_to_all(blocks, axis, 0, 0, tiled=True)  72.9 us
    all_gather x4, blocking collectives, ring_sum(): lax.all_gather(own.astype(jnp.bfloat16), axis, axis=0, tiled=True, axis_i...  20.7 us
    all_gather x1, blocking collectives, local(): lax.all_gather(last_joined(came, mismatch, jnp.concatenate([by_core, pad]...  14.7 us
    ppermute x1, starting transfers between devices, local(): student_other = lax.ppermute(student, 'core', [(0, 1), (1, 0)])  8.92 us
    dot_general x10, matrix products, product(): lax.dot_general(a, b, (((a_dim,), (b_dim,)), ((), ())), preferred_element...  7.84 us
    all_to_all x1, waiting for transfers between devices, exchange(): return lax.all_to_all(blocks, axis, 0, 0, tiled=True)  7.71 us
    all_to_all x1, starting transfers between devices, exchange(): return lax.all_to_all(blocks, axis, 0, 0, tiled=True)  3.41 us
  transfers between devices with their start and end apart: 2, of which 1 were waited for; matrix products, arithmetic and copies ran while one was open for 3% of the time, Pallas kernels for 0%

profile of v6, /device:TPU:1, one launch (start us, length us, event | category | flops | bytes accessed | tf_op | source)
XLA Modules:
  0.0 145.8 jit_solution(9658991247170403901)
XLA Ops:
  0.6 0.0 copy-start
  0.6 0.0 copy-start.7
  0.7 8.9 %collective-permute-start = (bf16[512,2048]{1,0:T(8,128)(2,1)}, bf16[512,2048]{1,0:T(8,128)(2,1)}, u32[]{:S(2)}, u32[]{:S(2)}) collective-permute-start(bf16[512,2048]{1,0:T(8,128)(2,1)} %param.3), channel_id=1, source_target_pairs={{0,1},{1,0},{2,3},{3,2},{4,5},{5,4},{6,7},{7,6},{8,9},{9,8},{10,11... | collective-permute-start | bytes 6291464 | tf_op jit(solution)/shard_map/ppermute | solution.py:126
  9.6 0.0 copy-done
  9.6 0.0 copy-start.4
  9.6 2.0 %fusion.7 = f32[128,512]{1,0:T(8,128)S(1)} fusion(bf16[2048,128]{1,0:T(8,128)(2,1)} %param.5, bf16[512,2048]{1,0:T(8,128)(2,1)S(1)} %copy-done), kind=kOutput, calls=%fused_computation.36 | convolution fusion | flops 268435456 | bytes 2883584 | tf_op jit(solution)/shard_map/dot_general | solution.py:103
  11.6 0.0 copy-done.7
  11.6 0.0 copy-done.4
  11.7 0.8 fusion
  12.5 2.2 %all_gather.18 = f32[256,512]{1,0:T(8,128)S(1)} all-gather(f32[128,512]{1,0:T(8,128)S(1)} %fusion), channel_id=1, replica_groups=mesh['x'=4,'y_hi'=4,'y_lo'=2,'z_lo'=2,'z_hi'=4,'core'=2] {'core'}, dimensions={0}, use_global_device_ids=true | all-gather | bytes 786432 | tf_op jit(solution)/shard_map/all_gather | solution.py:129
  14.7 0.0 collective-permute-done.src_ref
  14.7 1.6 %hold.1 = bf16[512,2048]{1,0:T(8,128)(2,1)S(1)} custom-call(bf16[512,2048]{1,0:T(8,128)(2,1)} %collective-permute-done.src_ref), custom_call_target="tpu_custom_call" | custom-call | tf_op jit(solution)/shard_map/hold/pallas_call | solution.py:43
  16.3 0.0 copy-start.1
  16.4 13.8 %all_to_all.35 = bf16[4,64,512]{2,1,0:T(8,128)(2,1)S(1)} all-to-all(bf16[4,64,512]{2,1,0:T(8,128)(2,1)S(1)} %broadcast_in_dim.10), channel_id=1, replica_groups=mesh['x'=4,'y_hi'=4,'y_lo'=2,'z_lo'=2,'z_hi'=4,'core'=2] {'z_hi'}, dimensions={0} | all-to-all | bytes 524288 | tf_op jit(solution)/shard_map/all_to_all | solution.py:18
  30.2 0.5 convolution_convert_fusion.3
  30.7 0.5 convolution_convert_fusion.2
  31.2 0.0 copy-done.1
  31.3 14.6 %all_to_all.36 = bf16[16,64,256]{2,1,0:T(8,128)(2,1)S(1)} all-to-all(bf16[16,64,256]{2,1,0:T(8,128)(2,1)S(1)} %pad_maximum_fusion), channel_id=1, replica_groups=mesh['x'=4,'y_hi'=4,'y_lo'=2,'z_lo'=2,'z_hi'=4,'core'=2] {'x','y_lo','z_..., dimensions={0} | all-to-all | bytes 1048576 | tf_op jit(solution)/shard_map/all_to_all | solution.py:18
  45.9 0.1 reduce_sum.85
  46.0 4.3 %all_gather.19 = bf16[128,256]{1,0:T(8,128)(2,1)S(1)} all-gather(bf16[64,256]{1,0:T(8,128)(2,1)S(1)} %reduce_sum.85), channel_id=1, replica_groups={{0,32},{64,96},{1,33},{65,97},{2,34},{66,98},{3,35},{67,99},{4,36},{68,..., dimensions={0}, use_global_device_ids=true | all-gather | bytes 98304 | tf_op jit(solution)/shard_map/all_gather | solution.py:31
  50.3 0.0 copy-start.5
  50.3 5.7 %all_gather.20 = bf16[128,256]{1,0:T(8,128)(2,1)S(1)} all-gather(bf16[64,256]{1,0:T(8,128)(2,1)S(1)} %reduce_sum.86), channel_id=1, replica_groups={{32,64},{96,0},{33,65},{97,1},{34,66},{98,2},{35,67},{99,3},{36,68},{10..., dimensions={0}, use_global_device_ids=true | all-gather | bytes 98304 | tf_op jit(solution)/shard_map/all_gather | solution.py:31
  56.1 12.4 %all_to_all.37 = bf16[16,64,256]{2,1,0:T(8,128)(2,1)S(1)} all-to-all(bf16[16,64,256]{2,1,0:T(8,128)(2,1)S(1)} %broadcast_in_dim.11), channel_id=1, replica_groups=mesh['x'=4,'y_hi'=4,'y_lo'=2,'z_lo'=2,'z_hi'=4,'core'=2] {'x','y_lo','z_..., dimensions={0} | all-to-all | bytes 1048576 | tf_op jit(solution)/shard_map/all_to_all | solution.py:18
  68.4 0.0 copy-start.2
  68.5 0.0 copy-done.5
  68.5 0.8 fusion.8
  69.3 0.7 copy-done.2
  70.0 0.8 fusion.2
  70.8 11.0 %all_to_all.38 = bf16[4,64,512]{2,1,0:T(8,128)(2,1)S(1)} all-to-all(bf16[4,64,512]{2,1,0:T(8,128)(2,1)S(1)} %broadcast_in_dim.12), channel_id=1, replica_groups=mesh['x'=4,'y_hi'=4,'y_lo'=2,'z_lo'=2,'z_hi'=4,'core'=2] {'z_hi'}, dimensions={0} | all-to-all | bytes 524288 | tf_op jit(solution)/shard_map/all_to_all | solution.py:18
  81.9 0.5 convolution_convert_fusion
  82.4 0.5 convolution_convert_fusion.1
  83.0 10.8 %all_to_all.39 = bf16[16,64,256]{2,1,0:T(8,128)(2,1)S(1)} all-to-all(bf16[16,64,256]{2,1,0:T(8,128)(2,1)S(1)} %pad_maximum_fusion.1), channel_id=1, replica_groups=mesh['x'=4,'y_hi'=4,'y_lo'=2,'z_lo'=2,'z_hi'=4,'core'=2] {'x','y_lo','z_..., dimensions={0} | all-to-all | bytes 1048576 | tf_op jit(solution)/shard_map/all_to_all | solution.py:18
  93.8 0.1 reduce_sum.89
  93.9 5.0 %all_gather.21 = bf16[128,256]{1,0:T(8,128)(2,1)S(1)} all-gather(bf16[64,256]{1,0:T(8,128)(2,1)S(1)} %reduce_sum.89), channel_id=1, replica_groups={{0,32},{64,96},{1,33},{65,97},{2,34},{66,98},{3,35},{67,99},{4,36},{68,..., dimensions={0}, use_global_device_ids=true | all-gather | bytes 98304 | tf_op jit(solution)/shard_map/all_gather | solution.py:31
  98.9 0.0 copy-start.6
  98.9 5.7 %all_gather.22 = bf16[128,256]{1,0:T(8,128)(2,1)S(1)} all-gather(bf16[64,256]{1,0:T(8,128)(2,1)S(1)} %reduce_sum.90), channel_id=1, replica_groups={{32,64},{96,0},{33,65},{97,1},{34,66},{98,2},{35,67},{99,3},{36,68},{10..., dimensions={0}, use_global_device_ids=true | all-gather | bytes 98304 | tf_op jit(solution)/shard_map/all_gather | solution.py:31
  104.6 10.4 %all_to_all.40 = bf16[16,64,256]{2,1,0:T(8,128)(2,1)S(1)} all-to-all(bf16[16,64,256]{2,1,0:T(8,128)(2,1)S(1)} %broadcast_in_dim.13), channel_id=1, replica_groups=mesh['x'=4,'y_hi'=4,'y_lo'=2,'z_lo'=2,'z_hi'=4,'core'=2] {'x','y_lo','z_..., dimensions={0} | all-to-all | bytes 1048576 | tf_op jit(solution)/shard_map/all_to_all | solution.py:18
  115.1 0.0 copy-start.3
  115.1 0.0 copy-done.6
  115.1 0.8 fusion.9
  115.9 0.7 copy-done.3
  116.6 0.8 convolution_add_fusion
  117.4 0.7 broadcast_in_dim.14
  118.1 3.4 %all-to-all-start.6 = ((bf16[4,64,512]{2,1,0:T(8,128)(2,1)}), bf16[4,64,512]{2,1,0:T(8,128)(2,1)S(1)}, u32[]{:S(2)}, u32[]{:S(2)}) async-start(bf16[4,64,512]{2,1,0:T(8,128)(2,1)} %broadcast_in_dim.14), calls=%async_computation.6 | async-start | bytes 524288 | tf_op jit(solution)/shard_map/all_to_all | solution.py:18
  121.6 0.1 add_bitcast_fusion.1
  121.7 0.1 maximum_select_fusion
  121.8 0.7 dynamic-slice_convert_fusion.panel_ref
  122.5 7.7 %all-to-all-done.6.got_ref = bf16[4,64,512]{2,1,0:T(8,128)(2,1)S(1)} async-done(((bf16[4,64,512]{2,1,0:T(8,128)(2,1)}), bf16[4,64,512]{2,1,0:T(8,128)(2,1)S(1)}, u32[]{:S(2)}, u32[]{:S(2)}) %all-to-all-start.6) | async-done | bytes 262176 | tf_op jit(solution)/shard_map/all_to_all | solution.py:18
  130.3 14.7 %all_gather.23.got_ref = f32[128,640]{1,0:T(8,128)S(1)} all-gather(f32[64,640]{1,0:T(8,128)S(1)} %last_joined.1), channel_id=1, replica_groups=mesh['x'=4,'y_hi'=4,'y_lo'=2,'z_lo'=2,'z_hi'=4,'core'=2] {'core'}, dimensions={0}, use_global_device_ids=true | all-gather | bytes 491520 | tf_op jit(solution)/shard_map/all_gather | solution.py:174
  145.0 0.8 finish.1
  (28 shorter events, 0.7 us)
Async XLA Ops:
  0.6 9.0 %copy-start = (bf16[512,2048]{1,0:T(8,128)(2,1)S(1)}, bf16[512,2048]{1,0:T(8,128)(2,1)}, u32[]{:S(2)}) copy-start(bf16[512,2048]{1,0:T(8,128)(2,1)} %param.4) | copy-start | bytes 6291460
  0.6 11.0 %copy-start.7 = (bf16[2048,128]{1,0:T(8,128)(2,1)S(1)}, bf16[2048,128]{1,0:T(8,128)(2,1)}, u32[]{:S(2)}) copy-start(bf16[2048,128]{1,0:T(8,128)(2,1)} %param.5) | copy-start | bytes 1572868
  0.7 14.0 %collective-permute-start = (bf16[512,2048]{1,0:T(8,128)(2,1)}, bf16[512,2048]{1,0:T(8,128)(2,1)}, u32[]{:S(2)}, u32[]{:S(2)}) collective-permute-start(bf16[512,2048]{1,0:T(8,128)(2,1)} %param.3), channel_id=1, source_target_pairs={{0,1},{1,0},{2,3},{3,2},{4,5},{5,4},{6,7},{7,6},{8,9},{9,8},{10,11... | collective-permute-start | bytes 6291464 | tf_op jit(solution)/shard_map/ppermute | solution.py:126
  9.6 2.0 %copy-start.4 = (bf16[512,2048]{1,0:T(8,128)(2,1)S(1)}, bf16[512,2048]{1,0:T(8,128)(2,1)}, u32[]{:S(2)}) copy-start(bf16[512,2048]{1,0:T(8,128)(2,1)} %param.3) | copy-start | bytes 6291460
  16.3 14.9 %copy-start.1 = (bf16[512,2048]{1,0:T(8,128)(2,1)}, bf16[512,2048]{1,0:T(8,128)(2,1)S(1)}, u32[]{:S(2)}) copy-start(bf16[512,2048]{1,0:T(8,128)(2,1)S(1)} %hold.1) | copy-start | bytes 6291460
  50.3 18.2 %copy-start.5 = (bf16[512,2048]{1,0:T(8,128)(2,1)S(1)}, bf16[512,2048]{1,0:T(8,128)(2,1)}, u32[]{:S(2)}) copy-start(bf16[512,2048]{1,0:T(8,128)(2,1)} %param.3) | copy-start | bytes 6291460
  68.4 1.6 %copy-start.2 = (bf16[512,2048]{1,0:T(8,128)(2,1)S(1)}, bf16[512,2048]{1,0:T(8,128)(2,1)}, u32[]{:S(2)}) copy-start(bf16[512,2048]{1,0:T(8,128)(2,1)} %copy-done.1) | copy-start | bytes 6291460
  98.9 16.3 %copy-start.6 = (bf16[512,2048]{1,0:T(8,128)(2,1)S(1)}, bf16[512,2048]{1,0:T(8,128)(2,1)}, u32[]{:S(2)}) copy-start(bf16[512,2048]{1,0:T(8,128)(2,1)} %param.3) | copy-start | bytes 6291460
  115.1 1.6 %copy-start.3 = (bf16[512,2048]{1,0:T(8,128)(2,1)S(1)}, bf16[512,2048]{1,0:T(8,128)(2,1)}, u32[]{:S(2)}) copy-start(bf16[512,2048]{1,0:T(8,128)(2,1)} %copy-done.1) | copy-start | bytes 6291460
  118.1 12.1 %all-to-all-start.6 = ((bf16[4,64,512]{2,1,0:T(8,128)(2,1)}), bf16[4,64,512]{2,1,0:T(8,128)(2,1)S(1)}, u32[]{:S(2)}, u32[]{:S(2)}) async-start(bf16[4,64,512]{2,1,0:T(8,128)(2,1)} %broadcast_in_dim.14), calls=%async_computation.6 | async-start | bytes 524288 | tf_op jit(solution)/shard_map/all_to_all | solution.py:18
